TPU v7x, 256 devices: a whole 4x4x8 slice. The times are simulated.
256 devices in a mesh: row: 32 (over y, x, core), col: 8 (over z).
Axes of the slice: x: 4, y: 4, z: 8, core: 2. Of those that a mesh axis runs over, the one named last changes fastest.
Arguments:
- tokens: bfloat16 [8192, 12288], P('row', 'col'), may hold values from -6 to 6
- weight_blocks: bfloat16 [96, 16, 128, 128], P('row', 'col'), may hold values from -0.1875 to 0.1875
- block_cols: int32 [96, 16], P(None, 'col'), may hold values from 0 to 23, as said below
- cotangent: bfloat16 [8192, 24576], P('row', 'col'), may hold values from -6 to 6
Outputs:
- activated: bfloat16 [8192, 24576], P('row', 'col')
- grad_tokens: bfloat16 [8192, 12288], P('row', 'col')
- grad_blocks: bfloat16 [96, 16, 128, 128], P('row', 'col')
Inputs may be any that keep to these rules, and one draw needn't show every extreme that they name: `block_cols`: within each block row and panel the 2 entries are different block columns; the first entry of panel p in block row k is (k + o_p) mod 24 for an offset o_p of the panel.
All inputs are finite; a program needn't handle non-finite values.
Results may differ from a plain program's by a relative error of at most 0.022.
Values may be sent and summed in bfloat16 or wider, within the bound.
A program may use at most 128 MiB of HBM per device.

v0:
```python
import jax
import jax.numpy as jnp
from jax import lax
from jax.sharding import PartitionSpec as P

PB = 24
KP = 2


def activate(values):
    return jax.nn.gelu(values, approximate=True)


def spread(products, select):
    high_part = products.astype(jnp.bfloat16)
    low_part = (products - high_part.astype(jnp.float32)).astype(jnp.bfloat16)
    upper = jnp.einsum("tksf,ksj->tjf", high_part, select, preferred_element_type=jnp.float32)
    lower = jnp.einsum("tksf,ksj->tjf", low_part, select, preferred_element_type=jnp.float32)
    return upper + lower


def on_device(tokens, weight_blocks, block_cols, cotangent):
    tok_rows = tokens.shape[0]
    block_size = weight_blocks.shape[3]
    slot_count = weight_blocks.shape[1]
    full_tokens = lax.all_gather(tokens, "col", axis=1, tiled=True)
    block_total = full_tokens.shape[1] // block_size
    token_blocks = full_tokens.reshape(tok_rows, block_total, block_size)
    width_blocks = slot_count // KP * PB
    local_cols = block_cols + (jnp.arange(slot_count, dtype=jnp.int32) // KP * PB)[None, :]
    onehot = local_cols[:, :, None] == jnp.arange(width_blocks, dtype=jnp.int32)[None, None, :]
    onehot_half = onehot.astype(jnp.bfloat16)
    weight_piece = lax.all_gather(weight_blocks, "row", axis=0, tiled=True)
    token_part = token_blocks
    products = jnp.einsum(
        "tkd,ksdf->tksf", token_part, weight_piece, preferred_element_type=jnp.float32
    )
    preact = spread(products, onehot_half)
    preact = preact.reshape(tok_rows, width_blocks * block_size)
    act_value, pullback = jax.vjp(activate, preact)
    grad_pre = pullback(cotangent.astype(jnp.float32))[0].astype(jnp.bfloat16)
    picked = jnp.einsum(
        "tjf,ksj->tksf",
        grad_pre.reshape(tok_rows, width_blocks, block_size),
        onehot_half,
        preferred_element_type=jnp.float32,
    ).astype(jnp.bfloat16)
    weight_piece = lax.all_gather(weight_blocks, "row", axis=0, tiled=True)
    row_count = weight_piece.shape[0]
    grad_part = picked
    result = jnp.einsum(
        "tksf,ksdf->tkd", grad_part, weight_piece, preferred_element_type=jnp.float32
    )
    partial_value = result.reshape(tok_rows, row_count * block_size)
    grad_tokens = lax.psum_scatter(
        partial_value.astype(jnp.bfloat16), "col", scatter_dimension=1, tiled=True
    )
    token_part = token_blocks
    grad_part = picked
    grad_blocks = lax.psum_scatter(
        jnp.einsum(
            "tkd,tksf->ksdf", token_part, grad_part, preferred_element_type=jnp.float32
        ).astype(jnp.bfloat16),
        "row",
        scatter_dimension=0,
        tiled=True,
    )
    return (act_value.astype(jnp.bfloat16), grad_tokens, grad_blocks)


def solution(mesh):
    return jax.shard_map(
        on_device,
        mesh=mesh,
        in_specs=(P("row", "col"), P("row", "col", None, None), P(None, "col"), P("row", "col")),
        out_specs=(P("row", "col"), P("row", "col"), P("row", "col", None, None)),
        check_vma=False,
    )
```

profile of v0, /device:TPU:2, one launch (start us, length us, event | category | flops | bytes accessed | tf_op | source)
XLA Modules:
  0.0 414.8 jit_solution(13909498882388379742)
XLA Ops:
  7.2 2.3 copy.26
  9.5 0.0 all-gather.3.cloned.1.call-start
  9.6 0.7 all-gather.3.cloned.1.call-update
  10.3 0.0 reduce-scatter.5.cloned.1.call-start
  10.3 0.8 broadcast_add_fusion
  11.1 76.7 %all-gather.5.cloned.1.call-done = bf16[256,12288]{0,1:T(8,128)(2,1)} async-done(((bf16[256,1536]{0,1:T(8,128)(2,1)}), bf16[256,12288]{0,1:T(8,128)(2,1)}) %all-gather.5.cloned.1.call-update) | async-done | bytes 6291472 | tf_op jit(solution)/shard_map/all_gather | solution.py:26
  87.8 54.6 %all-gather.3.cloned.1.call-done = bf16[96,2,128,128]{3,2,1,0:T(8,128)(2,1)} async-done(((bf16[3,2,128,128]{3,2,1,0:T(8,128)(2,1)}), bf16[96,2,128,128]{3,2,1,0:T(8,128)(2,1)}) %all-gather.3.cloned.1.call-update) | async-done | bytes 6291472 | tf_op jit(solution)/shard_map/all_gather | solution.py:33
  142.4 14.0 %fusion = (bf16[256,96,2,128]{0,3,2,1:T(8,128)(2,1)}, bf16[256,96,2,128]{0,3,2,1:T(8,128)(2,1)}) fusion(bf16[96,2,128,128]{3,2,1,0:T(8,128)(2,1)} %all-gather.3.cloned.1.call-done, bf16[256,96,128,1]{0,2,3,1:T(8,128)(2,1)} %bitcast.67), kind=kOutput, calls=%fused_computation.2 | convolution fusion | flops 1635778560 | bytes 37748736 | tf_op jit(solution)/shard_map/tkd,ksdf->tksf/dot_general | solution.py:35
  156.4 16.7 %copy.29 = bf16[256,96,2,128]{3,1,2,0:T(8,128)(2,1)} copy(bf16[256,96,2,128]{0,3,2,1:T(8,128)(2,1)} %get-tuple-element.13) | data formatting | bytes 25165824 | tf_op jit(solution)/shard_map/convert_element_type | solution.py:15
  173.0 16.8 %copy.30 = bf16[256,96,2,128]{3,1,2,0:T(8,128)(2,1)} copy(bf16[256,96,2,128]{0,3,2,1:T(8,128)(2,1)} %get-tuple-element.12) | data formatting | bytes 25165824 | tf_op jit(solution)/shard_map/convert_element_type | solution.py:16
  189.9 6.5 %fusion.16 = f32[24,256,128,1]{2,0,3,1:T(8,128)S(1)} fusion(bf16[256,96,2,128]{3,1,2,0:T(8,128)(2,1)} %copy.29, s32[96,2]{0,1:T(2,128)S(1)} %broadcast_add_fusion), kind=kOutput, calls=%fused_computation.27 | convolution fusion | flops 301994496 | bytes 15729408 | tf_op jit(solution)/shard_map/tksf,ksj->tjf/dot_general | solution.py:17
  196.4 1.6 copy-done
  198.0 1.8 bitcast_add_fusion
  199.9 3.5 fusion.12
  203.3 0.3 copy.48
  203.6 6.3 %convert_bitcast_fusion = bf16[256,96,2,128]{3,1,0,2:T(8,128)(2,1)} fusion(bf16[256,24,128,1]{2,1,0,3:T(8,128)(2,1)S(1)} %bitcast.70, s32[96,2]{0,1:T(2,128)S(1)} %broadcast_add_fusion), kind=kOutput, calls=%fused_computation.4 | convolution fusion | flops 308285952 | bytes 14156544 | tf_op jit(solution)/shard_map/tjf,ksj->tksf/dot_general | solution.py:42
  210.0 16.9 %copy.33 = bf16[256,96,2,128]{0,3,2,1:T(8,128)(2,1)} copy(bf16[256,96,2,128]{3,1,0,2:T(8,128)(2,1)} %convert_bitcast_fusion) | data formatting | bytes 25165824 | tf_op jit(solution)/shard_map/convert_element_type | solution.py:47
  226.8 9.9 %convert_bitcast_fusion.1 = bf16[96,2,128,128]{2,3,1,0:T(8,128)(2,1)} fusion(bf16[256,96,2,128]{0,3,2,1:T(8,128)(2,1)} %copy.33, bf16[256,96,128,1]{0,2,3,1:T(8,128)(2,1)} %bitcast.68), kind=kOutput, calls=%fused_computation.5 | convolution fusion | flops 1613758464 | bytes 25165824 | tf_op jit(solution)/shard_map/tkd,tksf->ksdf/dot_general | solution.py:61
  236.8 0.2 reduce-scatter.3.cloned.1.call-start
  237.0 11.3 %bitcast_convert_fusion.1 = bf16[96,256,128]{1,2,0:T(8,128)(2,1)} fusion(bf16[96,2,128,128]{3,2,1,0:T(8,128)(2,1)} %all-gather.3.cloned.1.call-done, bf16[256,96,2,128]{0,3,2,1:T(8,128)(2,1)} %copy.33), kind=kOutput, calls=%fused_computation.3 | convolution fusion | flops 1613758464 | bytes 25165824 | tf_op jit(solution)/shard_map/tksf,ksdf->tkd/dot_general | solution.py:51
  248.3 8.8 %copy.32 = bf16[256,12288]{1,0:T(8,128)(2,1)} copy(bf16[256,12288]{0,1:T(8,128)(2,1)} %bitcast.69) | data formatting | bytes 12582912 | tf_op jit(solution)/shard_map/convert_element_type | solution.py:56
  257.2 73.1 %reduce-scatter.5.cloned.1.call-done = bf16[3,2,128,128]{2,3,1,0:T(8,128)(2,1)} async-done(((bf16[96,2,128,128]{2,3,1,0:T(8,128)(2,1)}), bf16[3,2,128,128]{2,3,1,0:T(8,128)(2,1)}) %reduce-scatter.5.cloned.1.call-update) | async-done | bytes 196624 | tf_op jit(solution)/shard_map/reduce_scatter | solution.py:60
  330.3 1.7 copy.35
  332.0 76.2 %reduce-scatter.3.cloned.1.call-done = bf16[256,1536]{1,0:T(8,128)(2,1)} async-done(((bf16[256,12288]{1,0:T(8,128)(2,1)}), bf16[256,1536]{1,0:T(8,128)(2,1)}) %reduce-scatter.3.cloned.1.call-update) | async-done | bytes 786448 | tf_op jit(solution)/shard_map/reduce_scatter | solution.py:55
  (8 shorter events, 0.1 us)
Async XLA Ops:
  7.2 80.7 %all-gather.5.cloned.1.call-start = ((), (), s32[]{:S(2)}) async-start(), calls=%async_computation.3 | async-start | bytes 7077888 | tf_op jit(solution)/shard_map/all_gather | solution.py:26
  9.5 132.9 %all-gather.3.cloned.1.call-start = ((), (), s32[]{:S(2)}) async-start(), calls=%async_computation.2 | async-start | bytes 6488064 | tf_op jit(solution)/shard_map/all_gather | solution.py:33
  10.3 320.0 %reduce-scatter.5.cloned.1.call-start = ((), (), s32[]{:S(2)}) async-start(), calls=%async_computation.5 | async-start | bytes 6488064 | tf_op jit(solution)/shard_map/reduce_scatter | solution.py:60
  189.9 8.2 %copy-start = (bf16[256,96,2,128]{3,1,2,0:T(8,128)(2,1)S(1)}, bf16[256,96,2,128]{3,1,2,0:T(8,128)(2,1)}, u32[]{:S(2)}) copy-start(bf16[256,96,2,128]{3,1,2,0:T(8,128)(2,1)} %copy.30) | copy-start | bytes 37748740
  198.0 1.8 copy-start.1
  236.8 171.5 %reduce-scatter.3.cloned.1.call-start = ((), (), s32[]{:S(2)}) async-start(), calls=%async_computation.4 | async-start | bytes 7077888 | tf_op jit(solution)/shard_map/reduce_scatter | solution.py:55
Sparse Core Ops, SparseCore 0:
  10.4 77.4 all-gather.4
  90.4 51.9 all-gather.2
  236.9 93.3 reduce-scatter.4
  333.4 74.7 reduce-scatter.2
where the time goes:
time: 417 us; the launch traced here: 415 us
  waiting for transfers between devices  281 us (67%)
  local copies, waits for them, and re-layouts  65.1 us (16%)
  matrix products  49.9 us (12%)
  between operations  13.8 us (3%)
  other arithmetic  4.22 us (1%)
    all_gather x1, waiting for transfers between devices, on_device(): full_tokens = lax.all_gather(tokens, 'col', axis=1, tiled=True)  76.7 us
    reduce_scatter x1, waiting for transfers between devices, on_device(): lax.psum_scatter(partial_value.astype(jnp.bfloat16), 'col', scatter_dimen...  76.2 us
    reduce_scatter x1, waiting for transfers between devices, on_device(): lax.psum_scatter(jnp.einsum('tkd,tksf->ksdf', token_part, grad_part, pref...  73.1 us
    all_gather x1, waiting for transfers between devices, on_device(): weight_piece = lax.all_gather(weight_blocks, 'row', axis=0, tiled=True)  54.6 us
    convert_element_type x1, local copies, waits for them, and re-layouts, on_device(): picked = jnp.einsum('tjf,ksj->tksf', grad_pre.reshape(tok_rows, width_blo...  16.9 us
    convert_element_type x1, local copies, waits for them, and re-layouts, spread(): low_part = (products - high_part.astype(jnp.float32)).astype(jnp.bfloat16)  16.8 us
    convert_element_type x1, local copies, waits for them, and re-layouts, spread(): high_part = products.astype(jnp.bfloat16)  16.7 us
    dot_general x1, matrix products, on_device(): jnp.einsum('tkd,ksdf->tksf', token_part, weight_piece, preferred_element_...  14 us
  transfers between devices with their start and end apart: 4, of which 4 were waited for; matrix products, arithmetic and copies ran while one was open for 5% of the time, Pallas kernels for 0%

commit v1 on v0

v1 whole, which is shorter than its diff:
```python
import jax
import jax.numpy as jnp
from jax import lax
from jax.experimental import pallas as pl
from jax.experimental.pallas import tpu as pltpu
from jax.sharding import PartitionSpec as P

MESH = pl.DeviceIdType.MESH
F32 = jnp.float32
BF16 = jnp.bfloat16

BLK = 128
PB = 24
KP = 2
DB = 96
NX = 4
NZ = 8
ENT = DB * KP
PAIRS = (ENT + PB) // 2
CHUNKS = 2
T = 128
FEAT = 1536
FB = FEAT // BLK
NP = 2
PW = FEAT // NP
HALF = T // 2

AT_K = 0
AT_W = AT_K + 2 * PAIRS
AT_KEEP = AT_W + 2 * PAIRS
AT_LAST = AT_KEEP + PAIRS
AT_COL = AT_LAST + PB
AT_END = AT_COL + ENT


def weight_position(k):
    r, i = k // 3, k % 3
    core = r % 2
    x = (r // 2) % NX
    y = r // (2 * NX)
    a = x + (y - x) * core
    b = y + (x - y) * core
    return (((core * NX + a) * NX + b) * 3 + i) * 2


def plan(cols):
    c = cols.reshape(ENT)
    e = jnp.arange(ENT, dtype=jnp.int32)
    j = jnp.arange(PB, dtype=jnp.int32)
    hit = (c[:, None] == j[None, :]).astype(jnp.int32)
    count = jnp.sum(hit, axis=0)
    pairs = (count + 1) // 2
    base = jnp.sum(jnp.where(j[None, :] < j[:, None], pairs[None, :], 0), axis=1)
    rank = jnp.sum(((c[:, None] == c[None, :]) & (e[None, :] < e[:, None])).astype(jnp.int32), axis=1)
    at = jnp.sum(hit * (2 * base)[None, :], axis=1) + rank
    slot = jnp.arange(2 * PAIRS, dtype=jnp.int32)
    entry = jnp.sum(jnp.where(at[None, :] == slot[:, None], e[None, :] + 1, 0), axis=1) - 1
    row = jnp.maximum(entry, 0) // 2
    where = jnp.where(entry < 0, ENT, weight_position(row) + entry % 2)
    pair = jnp.arange(PAIRS, dtype=jnp.int32)
    keep = 1 - jnp.max((base[None, :] == pair[:, None]).astype(jnp.int32), axis=1)
    last = base + pairs - 1
    return jnp.concatenate([row, where, keep, last, c])


def kernel(
    idx, tok_hbm, w_hbm, cot_hbm,
    act_hbm, gt_hbm, gb_hbm,
    tok0, tok1, wg, seg, cot, act, gp0, gp1, dx0, dx1, rs0, rs1, dw, pr, bufa, bufb,
    load_sem, out_sem, ag_send_sem, ag_recv_sem, rs_send_sem, rs_recv_sem,
    wb_send, wb_recv, wa_send, wa_recv, wc_send, wc_recv,
    gc_send, gc_recv, ga_send, ga_recv, gb_send, gb_recv,
):
    toks, gps, dxs, rss = (tok0, tok1), (gp0, gp1), (dx0, dx1), (rs0, rs1)
    row, c = lax.axis_index("row"), lax.axis_index("col")
    core = row % 2
    x = (row // 2) % NX
    y = row // (2 * NX)
    a = x + (y - x) * core
    b = y + (x - y) * core

    def ring(v, step, n):
        return lax.rem(v + step + n, n)

    def chip(a_, b_):
        x_ = a_ + (b_ - a_) * core
        y_ = b_ + (a_ - b_) * core
        return ((y_ * NX + x_) * 2 + core, c)

    z_to = ((row, ring(c, 1, NZ)), (row, ring(c, -1, NZ)))
    a_to = (chip(ring(a, 1, NX), b), chip(ring(a, -1, NX), b))
    b_to = (chip(a, ring(b, 1, NX)), chip(a, ring(b, -1, NX)))
    sibling = (row + 1 - 2 * core, c)

    started = []

    def remote(src, dst, send, recv, to):
        return pltpu.make_async_remote_copy(
            src_ref=src, dst_ref=dst, send_sem=send, recv_sem=recv, device_id=to, device_id_type=MESH
        )

    def send(src, dst, send_sem, recv_sem, to):
        copy = remote(src, dst, send_sem, recv_sem, to)
        copy.start()
        started.append(copy)

    w_load = pltpu.make_async_copy(w_hbm, wg.at[pl.ds(((core * NX + a) * NX + b) * 6, 6)], load_sem.at[2])
    cot_load = pltpu.make_async_copy(cot_hbm, cot, load_sem.at[3])

    def tok_load(h):
        for i in range(FB):
            pltpu.make_async_copy(
                tok_hbm.at[pl.ds(h * T, T), pl.ds(i * BLK, BLK)], toks[h].at[c * FB + i], load_sem.at[h]
            ).start()

    def tok_wait(h):
        region = toks[h].at[pl.ds(c * FB, FB)]
        pltpu.make_async_copy(region, region, load_sem.at[h]).wait()

    tok_load(0)
    w_load.start()
    tok_load(1)
    cot_load.start()

    barrier = pltpu.get_barrier_semaphore()
    for to in (*z_to, *a_to, *b_to, sibling):
        pl.semaphore_signal(barrier, inc=1, device_id=to, device_id_type=MESH)
    pl.semaphore_wait(barrier, 7)

    def ag_region(h, shard, way, step, p):
        rows = pl.ds(0, T) if step < 4 else pl.ds(way * HALF, HALF)
        return toks[h].at[pl.ds(shard * FB + p * (FB // NP), FB // NP), rows]

    def ag_send(h, way, step, p):
        shard = ring(c, (1 - step) if way == 0 else (step - 1), NZ)
        region = ag_region(h, shard, way, step, p)
        sem = (h, way, step - 1, p)
        send(region, region, ag_send_sem.at[sem], ag_recv_sem.at[sem], z_to[way])

    def ag_event(h, step, p):
        for way in range(2):
            shard = ring(c, -step if way == 0 else step, NZ)
            region = ag_region(h, shard, way, step, p)
            sem = (h, way, step - 1, p)
            remote(region, region, ag_send_sem.at[sem], ag_recv_sem.at[sem], z_to[way]).wait_recv()
            if step < 4:
                ag_send(h, way, step + 1, p)

    def ag_open(h):
        for p in range(NP):
            for way in range(2):
                ag_send(h, way, 1, p)

    def w_region(core_, a_, b_, lo=0, n=6):
        return wg.at[pl.ds(((core_ * NX + a_) * NX + b_) * 6 + lo, n)]

    def b_of(q):
        return ring(b, (0, 1, -1, 2)[q], NX)

    def w_to_a(q):
        region = w_region(core, a, b_of(q))
        for way in range(2):
            send(region, region, wa_send.at[way, 0, q], wa_recv.at[way, 0, q], a_to[way])

    def w_to_sibling(g, q):
        region = w_region(core, ring(a, (0, 1, -1, 2)[g], NX), b_of(q))
        send(region, region, wc_send.at[g, q], wc_recv.at[g, q], sibling)

    def w_open():
        region = w_region(core, a, b)
        for way in range(2):
            send(region, region, wb_send.at[way, 0], wb_recv.at[way, 0], b_to[way])
        w_to_a(0)
        w_to_sibling(0, 0)

    def w_wait(region, send_sem, recv_sem, to):
        remote(region, region, send_sem, recv_sem, to).wait_recv()

    def w_near_b():
        for way in range(2):
            q = 2 if way == 0 else 1
            w_wait(w_region(core, a, b_of(q)), wb_send.at[way, 0], wb_recv.at[way, 0], b_to[way])
            region = w_region(core, a, b_of(q), 3 * way, 3)
            send(region, region, wb_send.at[way, 1], wb_recv.at[way, 1], b_to[way])
            w_to_a(q)
            w_to_sibling(0, q)

    def w_far_b():
        for way in range(2):
            w_wait(w_region(core, a, b_of(3), 3 * way, 3), wb_send.at[way, 1], wb_recv.at[way, 1], b_to[way])
        w_to_a(3)
        w_to_sibling(0, 3)

    def w_near_a(q):
        for way in range(2):
            g = 2 if way == 0 else 1
            a_ = ring(a, -1 if way == 0 else 1, NX)
            w_wait(w_region(core, a_, b_of(q)), wa_send.at[way, 0, q], wa_recv.at[way, 0, q], a_to[way])
            region = w_region(core, a_, b_of(q), 3 * way, 3)
            send(region, region, wa_send.at[way, 1, q], wa_recv.at[way, 1, q], a_to[way])
            w_to_sibling(g, q)

    def w_far_a(q):
        a_ = ring(a, 2, NX)
        for way in range(2):
            w_wait(w_region(core, a_, b_of(q), 3 * way, 3), wa_send.at[way, 1, q], wa_recv.at[way, 1, q], a_to[way])
        w_to_sibling(3, q)

    def w_close():
        for g in range(4):
            for q in range(4):
                a_ = ring(b, (0, 1, -1, 2)[g], NX)
                b_ = ring(a, (0, 1, -1, 2)[q], NX)
                w_wait(w_region(1 - core, a_, b_), wc_send.at[g, q], wc_recv.at[g, q], sibling)

    def lanes(k):
        return pl.ds(pl.multiple_of(k * BLK, BLK), BLK)

    def fwd(h, lo, hi):
        tok = toks[h]

        def body(i, acc):
            xs = jnp.concatenate([tok[idx[AT_K + 2 * i + s]] for s in range(2)], axis=1)
            ws = jnp.concatenate([wg[idx[AT_W + 2 * i + s]] for s in range(2)], axis=0)
            acc = acc * idx[AT_KEEP + i].astype(F32) + jnp.dot(xs, ws, preferred_element_type=F32)
            seg[i] = acc
            return acc

        start = jnp.zeros((T, BLK), F32) if lo == 0 else seg[lo - 1]
        lax.fori_loop(lo, hi, body, start, unroll=3)

    def gelu(h):
        rows = pl.ds(h * T, T)

        def body(j, carry):
            v = seg[idx[AT_LAST + j]]
            k0 = 0.7978845608028654
            v2 = v * v
            th = jnp.tanh(k0 * (v + 0.044715 * (v2 * v)))
            half = 0.5 * (1.0 + th)
            slope = half + (0.5 * v) * (1.0 - th * th) * (k0 * (1.0 + 3 * 0.044715 * v2))
            act[rows, lanes(j)] = (v * half).astype(BF16)
            gps[h][j] = (cot[rows, lanes(j)].astype(F32) * slope).astype(BF16)
            return carry

        lax.fori_loop(0, PB, body, 0)
        pltpu.make_async_copy(act.at[rows], act_hbm.at[rows], out_sem.at[h]).start()

    def grad_x(h, shard):
        gp, dx = gps[h], dxs[h]

        def body(i, carry):
            k = shard * (FB) + i
            at = weight_position(k)
            gs = jnp.concatenate([gp[idx[AT_COL + 2 * k + s]] for s in range(2)], axis=1)
            ws = jnp.concatenate([wg[at + s] for s in range(2)], axis=1)
            out = lax.dot_general(gs, ws, (((1,), (1,)), ((), ())), preferred_element_type=F32)
            dx[:, lanes(k)] = out.astype(BF16)
            return carry

        lax.fori_loop(0, FB, body, 0, unroll=3)

    def grad_w(core_, a_):
        def body(i, carry):
            b_, j = i // 3, i % 3
            at = (((core_ * NX + a_) * NX + b_) * 3 + j) * 2
            x_ = a_ + (b_ - a_) * core_
            y_ = b_ + (a_ - b_) * core_
            k = ((y_ * NX + x_) * 2 + core_) * 3 + j
            xs = jnp.concatenate([tok[k] for tok in toks], axis=0)
            cols = [idx[AT_COL + 2 * k + s] for s in range(2)]
            gs = jnp.concatenate(
                [jnp.concatenate([gp[col] for gp in gps], axis=0) for col in cols], axis=1
            )
            out = lax.dot_general(xs, gs, (((0,), (0,)), ((), ())), preferred_element_type=F32)
            dw[at] = out[:, :BLK].astype(BF16)
            dw[at + 1] = out[:, BLK:].astype(BF16)
            return carry

        lax.fori_loop(0, 12, body, 0, unroll=2)

    def rs_rows(way, step):
        return pl.ds(0, HALF) if step == 1 else pl.ds(HALF + (step - 2) * T, T)

    def rs_send(h, way, step, p):
        shard = ring(c, (5 - step) if way == 0 else (step - 5), NZ)
        col = pl.ds(pl.multiple_of(shard * FEAT + p * PW, PW), PW)
        rows = pl.ds(way * HALF, HALF) if step == 1 else pl.ds(0, T)
        sem = (h, way, step - 1, p)
        send(
            dxs[h].at[rows, col],
            rss[h].at[way, rs_rows(way, step), pl.ds(p * PW, PW)],
            rs_send_sem.at[sem],
            rs_recv_sem.at[sem],
            z_to[way],
        )

    def rs_open(h):
        for p in range(NP):
            for way in range(2):
                rs_send(h, way, 1, p)

    def rs_wait(h, way, step, p):
        region = rss[h].at[way, rs_rows(way, step), pl.ds(p * PW, PW)]
        sem = (h, way, step - 1, p)
        remote(region, region, rs_send_sem.at[sem], rs_recv_sem.at[sem], z_to[way]).wait_recv()

    def rs_event(h, step, p):
        dx, rs = dxs[h], rss[h]
        if step < 4:
            for way in range(2):
                rs_wait(h, way, step, p)
                shard = ring(c, (4 - step) if way == 0 else (step - 4), NZ)
                rows = pl.ds(way * HALF, HALF) if step == 1 else pl.ds(0, T)

                def body(i, carry):
                    at = lanes(shard * (FB) + p * (PW // BLK) + i)
                    got = rs[way, rs_rows(way, step), lanes(p * (PW // BLK) + i)]
                    dx[rows, at] = (dx[rows, at].astype(F32) + got.astype(F32)).astype(BF16)
                    return carry

                lax.fori_loop(0, PW // BLK, body, 0, unroll=2)
                rs_send(h, way, step + 1, p)
        else:
            for way in range(2):
                rs_wait(h, way, step, p)

            def body(i, carry):
                at = lanes(c * (FB) + p * (PW // BLK) + i)
                total = dx[:, at].astype(F32)
                for way in range(2):
                    total += rs[way, rs_rows(way, 4), lanes(p * (PW // BLK) + i)].astype(F32)
                dx[:, at] = total.astype(BF16)
                return carry

            lax.fori_loop(0, PW // BLK, body, 0, unroll=2)
            pltpu.make_async_copy(
                dx.at[:, pl.ds(pl.multiple_of(c * FEAT + p * PW, PW), PW)],
                gt_hbm.at[pl.ds(h * T, T), pl.ds(p * PW, PW)],
                out_sem.at[2 + h * NP + p],
            ).start()

    def w_at(a_, b_=0):
        return ((core * NX + a_) * NX + b_) * 6

    def pair_send(a_):
        src = dw.at[pl.ds((((1 - core) * NX + a_) * NX) * 6, 24)]
        send(src, pr.at[pl.ds(a_ * 24, 24)], gc_send.at[a_], gc_recv.at[a_], sibling)

    def add_blocks(dst, n, *srcs):
        def body(i, carry):
            total = dw[dst + i].astype(F32)
            for ref, at in srcs:
                total += ref[at + i].astype(F32)
            dw[dst + i] = total.astype(BF16)
            return carry

        lax.fori_loop(0, n, body, 0, unroll=2)

    def pair_add(a_):
        region = pr.at[pl.ds(a_ * 24, 24)]
        remote(region, region, gc_send.at[a_], gc_recv.at[a_], sibling).wait_recv()
        add_blocks(w_at(a_), 24, (pr, a_ * 24))

    def hop(buf, way, step, size, src, sems, to):
        off = way * (size + size // 2) + (0 if step == 0 else size // 2)
        n = size // 2 if step == 0 else size
        dst = buf.at[pl.ds(off, n)]
        return remote(dw.at[pl.ds(src, n)], dst, sems[0].at[way, step], sems[1].at[way, step], to), off

    def ring_open(buf, far, size, sems, tos):
        for way in range(2):
            copy, _ = hop(buf, way, 0, size, far + way * (size // 2), sems, tos[way])
            copy.start()
            started.append(copy)

    def ring_middle(buf, nexts, size, sems, tos):
        for way in range(2):
            copy, off = hop(buf, way, 0, size, 0, sems, tos[way])
            copy.wait_recv()
            add_blocks(nexts[way] + way * (size // 2), size // 2, (buf, off))
            copy, _ = hop(buf, way, 1, size, nexts[way], sems, tos[way])
            copy.start()
            started.append(copy)

    def ring_close(buf, own, size, sems, tos):
        srcs = []
        for way in range(2):
            copy, off = hop(buf, way, 1, size, 0, sems, tos[way])
            copy.wait_recv()
            srcs.append((buf, off))
        add_blocks(own, size, *srcs)

    a_sems, b_sems = (ga_send, ga_recv), (gb_send, gb_recv)
    a_near = (w_at(ring(a, 1, NX)), w_at(ring(a, -1, NX)))
    b_near = (w_at(a, ring(b, 1, NX)), w_at(a, ring(b, -1, NX)))

    wg[ENT] = jnp.zeros((BLK, BLK), BF16)
    tok_wait(0)
    ag_open(0)
    w_load.wait()
    w_open()
    w_near_b()
    w_near_a(0)
    w_far_b()
    ag_event(0, 1, 0)
    w_near_a(1)
    w_near_a(2)
    ag_event(0, 1, 1)
    w_near_a(3)
    w_far_a(0)
    w_far_a(1)
    w_far_a(2)
    ag_event(0, 2, 0)
    w_far_a(3)
    ag_event(0, 2, 1)
    ag_event(0, 3, 0)
    tok_wait(1)
    ag_event(0, 3, 1)
    ag_open(1)
    cot_load.wait()
    w_close()
    ag_event(0, 4, 0)
    ag_event(0, 4, 1)

    quarter = PAIRS // 4
    fwd(0, 0, quarter)
    ag_event(1, 1, 0)
    fwd(0, quarter, 2 * quarter)
    ag_event(1, 1, 1)
    fwd(0, 2 * quarter, 3 * quarter)
    fwd(0, 3 * quarter, PAIRS)
    ag_event(1, 2, 0)
    gelu(0)
    grad_x(0, ring(c, 4, NZ))
    ag_event(1, 2, 1)
    grad_x(0, ring(c, 3, NZ))
    grad_x(0, ring(c, -3, NZ))
    grad_x(0, ring(c, 2, NZ))
    ag_event(1, 3, 0)
    grad_x(0, ring(c, -2, NZ))
    grad_x(0, ring(c, 1, NZ))
    grad_x(0, ring(c, -1, NZ))
    grad_x(0, c)
    ag_event(1, 3, 1)
    rs_open(0)
    ag_event(1, 4, 0)
    ag_event(1, 4, 1)

    fwd(1, 0, quarter)
    rs_event(0, 1, 0)
    rs_event(0, 1, 1)
    fwd(1, quarter, 2 * quarter)
    fwd(1, 2 * quarter, 3 * quarter)
    rs_event(0, 2, 0)
    fwd(1, 3 * quarter, PAIRS)
    rs_event(0, 2, 1)
    gelu(1)
    grad_x(1, ring(c, 4, NZ))
    rs_open(1)
    grad_x(1, ring(c, 3, NZ))
    grad_x(1, ring(c, -3, NZ))
    rs_event(0, 3, 0)
    grad_x(1, ring(c, 2, NZ))
    grad_x(1, ring(c, -2, NZ))
    rs_event(0, 3, 1)
    rs_event(1, 1, 0)
    grad_x(1, ring(c, 1, NZ))
    grad_x(1, ring(c, -1, NZ))
    rs_event(1, 1, 1)
    grad_x(1, c)
    for g in range(2):
        grad_w(1 - core, g)
        pair_send(g)
    rs_event(0, 4, 0)
    for g in range(2, 4):
        grad_w(1 - core, g)
        pair_send(g)
    rs_event(0, 4, 1)
    rs_event(1, 2, 0)
    grad_w(core, ring(a, 2, NX))
    grad_w(core, ring(a, 1, NX))
    pair_add(ring(a, 2, NX))
    ring_open(bufa, w_at(ring(a, 2, NX)), 24, a_sems, a_to)
    rs_event(1, 2, 1)
    grad_w(core, ring(a, -1, NX))
    grad_w(core, a)
    pair_add(ring(a, 1, NX))
    pair_add(ring(a, -1, NX))
    pair_add(a)
    ring_middle(bufa, a_near, 24, a_sems, a_to)
    rs_event(1, 3, 0)
    ring_close(bufa, w_at(a), 24, a_sems, a_to)
    ring_open(bufb, w_at(a, ring(b, 2, NX)), 6, b_sems, b_to)
    rs_event(1, 3, 1)
    ring_middle(bufb, b_near, 6, b_sems, b_to)
    ring_close(bufb, w_at(a, b), 6, b_sems, b_to)
    last = pltpu.make_async_copy(dw.at[pl.ds(w_at(a, b), 6)], gb_hbm, out_sem.at[2 + CHUNKS * NP])
    last.start()
    rs_event(1, 4, 0)
    rs_event(1, 4, 1)

    last.wait()
    for h in range(CHUNKS):
        rows = pl.ds(h * T, T)
        pltpu.make_async_copy(act.at[rows], act_hbm.at[rows], out_sem.at[h]).wait()
        for p in range(NP):
            pltpu.make_async_copy(
                dxs[h].at[:, pl.ds(pl.multiple_of(c * FEAT + p * PW, PW), PW)],
                gt_hbm.at[pl.ds(h * T, T), pl.ds(p * PW, PW)],
                out_sem.at[2 + h * NP + p],
            ).wait()
    for copy in started:
        copy.wait_send()


def on_device(tokens, weight_blocks, block_cols, cotangent):
    idx = plan(block_cols)
    any_space = pl.BlockSpec(memory_space=pl.ANY)
    dma = pltpu.SemaphoreType.DMA
    act, grad_tokens, grad_blocks = pl.pallas_call(
        kernel,
        out_shape=(
            jax.ShapeDtypeStruct((CHUNKS * T, PB * BLK), BF16),
            jax.ShapeDtypeStruct((CHUNKS * T, FEAT), BF16),
            jax.ShapeDtypeStruct((6, BLK, BLK), BF16),
        ),
        in_specs=[pl.BlockSpec(memory_space=pltpu.SMEM), any_space, any_space, any_space],
        out_specs=(any_space, any_space, any_space),
        scratch_shapes=[
            pltpu.VMEM((DB, T, BLK), BF16),
            pltpu.VMEM((DB, T, BLK), BF16),
            pltpu.VMEM((ENT + 1, BLK, BLK), BF16),
            pltpu.VMEM((PAIRS, T, BLK), F32),
            pltpu.VMEM((CHUNKS * T, PB * BLK), BF16),
            pltpu.VMEM((CHUNKS * T, PB * BLK), BF16),
            pltpu.VMEM((PB, T, BLK), BF16),
            pltpu.VMEM((PB, T, BLK), BF16),
            pltpu.VMEM((T, DB * BLK), BF16),
            pltpu.VMEM((T, DB * BLK), BF16),
            pltpu.VMEM((2, HALF + 3 * T, FEAT), BF16),
            pltpu.VMEM((2, HALF + 3 * T, FEAT), BF16),
            pltpu.VMEM((ENT, BLK, BLK), BF16),
            pltpu.VMEM((ENT // 2, BLK, BLK), BF16),
            pltpu.VMEM((2 * 36, BLK, BLK), BF16),
            pltpu.VMEM((2 * 9, BLK, BLK), BF16),
            dma((4,)),
            dma((2 + CHUNKS * NP + 1,)),
            dma((CHUNKS, 2, 4, NP)),
            dma((CHUNKS, 2, 4, NP)),
            dma((CHUNKS, 2, 4, NP)),
            dma((CHUNKS, 2, 4, NP)),
            dma((2, 2)),
            dma((2, 2)),
            dma((2, 2, 4)),
            dma((2, 2, 4)),
            dma((4, 4)),
            dma((4, 4)),
            dma((4,)),
            dma((4,)),
            dma((2, 2)),
            dma((2, 2)),
            dma((2, 2)),
            dma((2, 2)),
        ],
        compiler_params=pltpu.CompilerParams(
            collective_id=0, has_side_effects=True, vmem_limit_bytes=60 * 1024 * 1024
        ),
        cost_estimate=pl.CostEstimate(flops=4_831_838_208, bytes_accessed=6_000_000, transcendentals=786_432),
    )(idx, tokens, weight_blocks.reshape(6, BLK, BLK), cotangent)
    return act, grad_tokens, grad_blocks.reshape(3, KP, BLK, BLK)


def solution(mesh):
    return jax.shard_map(
        on_device,
        mesh=mesh,
        in_specs=(P("row", "col"), P("row", "col", None, None), P(None, "col"), P("row", "col")),
        out_specs=(P("row", "col"), P("row", "col"), P("row", "col", None, None)),
        check_vma=False,
    )
```

time: 417 us -> 157 us (0.38)
  waiting for transfers between devices: 281 us -> 0 us
  Pallas kernels: 0 us -> 149 us
  local copies, waits for them, and re-layouts: 65.1 us -> 5.88 us
  matrix products: 49.9 us -> 0 us
  between operations: 13.8 us -> 0.71 us
    reduce_scatter x2 -> x0, waiting for transfers between devices: 149 us -> none  [the longest x1 76.2 us: on_device(): lax.psum_scatter(partial_value.astype(jnp.bfloat16), 'col', scatter_dimen...]
    pallas_call x0 -> x1, Pallas kernels: none -> 149 us  [on_device(): pl.pallas_call(kernel, out_shape=(jax.ShapeDtypeStruct((CHUNKS * T, PB *...]
    all_gather x2 -> x0, waiting for transfers between devices: 131 us -> none  [the longest x1 76.7 us: on_device(): full_tokens = lax.all_gather(tokens, 'col', axis=1, tiled=True)]
    convert_element_type x4 -> x0, local copies, waits for them, and re-layouts: 59.2 us -> none  [the longest x1 16.9 us: on_device(): picked = jnp.einsum('tjf,ksj->tksf', grad_pre.reshape(tok_rows, width_blo...]
    dot_general x6 -> x0, matrix products: 49.9 us -> none  [the longest x1 14 us: on_device(): jnp.einsum('tkd,ksdf->tksf', token_part, weight_piece, preferred_element_...]
  transfers between devices with their start and end apart: 4 -> 0, of which waited for: 4 -> 0; matrix products, arithmetic and copies ran while one was open for 5% -> 0% of each run, Pallas kernels for 0% -> 0%
where the time goes in v1:
time: 157 us; the launch traced here: 156 us
  Pallas kernels  149 us (95%)
  local copies, waits for them, and re-layouts  5.88 us (4%)
    pallas_call x1, Pallas kernels, on_device(): pl.pallas_call(kernel, out_shape=(jax.ShapeDtypeStruct((CHUNKS * T, PB *...  149 us
    unnamed x8, local copies, waits for them, and re-layouts  5.08 us

profile of v1, /device:TPU:2, one launch (start us, length us, event | category | flops | bytes accessed | tf_op | source)
XLA Modules:
  0.0 156.0 jit_solution(8615170366338184945)
XLA Ops:
  0.6 0.8 copy.8
  1.4 0.1 eq.59
  1.6 0.1 convert_reduce_fusion.1
  1.7 0.1 select_reduce_fusion.2
  1.8 0.1 convert_reduce_fusion.2
  1.9 0.1 select_reduce_fusion.1
  2.0 0.2 convert_reduce_fusion
  2.2 0.1 select_reduce_fusion
  2.4 0.7 concatenate.3.idx
  3.1 148.6 %shard_map.67 = (bf16[256,3072]{1,0:T(8,128)(2,1)}, bf16[256,1536]{1,0:T(8,128)(2,1)}, bf16[6,128,128]{2,1,0:T(8,128)(2,1)}) custom-call(s32[756]{0:T(1024)} %concatenate.3.idx, bf16[256,1536]{1,0:T(8,128)(2,1)} %tok_hbm.1, bf16[6,128,128]{2,1,0:T(8,128)(2,1)} %bitcast.3, bf16[256,3072]{1,0:T(8,128)(2,1)} %cot_hbm.1), custom_call_target="tpu_custom_call" | custom-call | flops 4831838208 | bytes 6000000 | tf_op jit(solution)/shard_map/pallas_call | solution.py:521
  151.6 0.0 copy-start
  151.7 0.0 copy-start.1
  151.7 2.7 %copy.12 = bf16[256,3072]{1,0:T(8,128)(2,1)} copy(bf16[256,3072]{1,0:T(8,128)(2,1)} %get-tuple-element.16) | data formatting | bytes 3145728
  154.4 0.0 copy-done
  154.4 0.9 copy.13
  155.3 0.0 copy-done.1
  155.3 0.7 copy.14
  (6 shorter events, 0.1 us)
Async XLA Ops:
  151.6 2.8 %copy-start = (bf16[256,1536]{1,0:T(8,128)(2,1)S(1)}, bf16[256,1536]{1,0:T(8,128)(2,1)}, u32[]{:S(2)}) copy-start(bf16[256,1536]{1,0:T(8,128)(2,1)} %get-tuple-element.17) | copy-start | bytes 2359300
  151.7 3.6 %copy-start.1 = (bf16[6,128,128]{2,1,0:T(8,128)(2,1)S(1)}, bf16[6,128,128]{2,1,0:T(8,128)(2,1)}, u32[]{:S(2)}) copy-start(bf16[6,128,128]{2,1,0:T(8,128)(2,1)} %get-tuple-element.8) | copy-start | bytes 589828

commit v2 on v1

v2 whole, which is shorter than its diff:
```python
import jax
import jax.numpy as jnp
from jax import lax
from jax.experimental import pallas as pl
from jax.experimental.pallas import tpu as pltpu
from jax.sharding import PartitionSpec as P

MESH = pl.DeviceIdType.MESH
F32 = jnp.float32
BF16 = jnp.bfloat16

BLK = 128
PB = 24
KP = 2
DB = 96
NX = 4
NZ = 8
ENT = DB * KP
PAIRS = (ENT + PB) // 2
CHUNKS = 2
T = 128
FEAT = 1536
FB = FEAT // BLK
NP = 2
PW = FEAT // NP
HALF = T // 2

TAB_K, TAB_KEEP, TAB_LAST, TAB_W = 0, 8, 16, 24


def weight_position(k):
    r, i = k // 3, k % 3
    core = r % 2
    x = (r // 2) % NX
    y = r // (2 * NX)
    a = x + (y - x) * core
    b = y + (x - y) * core
    return (((core * NX + a) * NX + b) * 3 + i) * 2


def kernel(
    cols_hbm, tok_hbm, w_hbm, cot_hbm,
    act_hbm, gt_hbm, gb_hbm,
    tok0, tok1, wg, seg, cot, act, gp0, gp1, dx0, dx1, rs0, rs1, dw, pr, bufa, bufb,
    cols_v, cols, count_v, count, place_v, place, tab_v, tab,
    load_sem, out_sem, send_sem, ag_sem, rs_sem, wb_sem, wa_sem, wc_sem, gc_sem, ga_sem, gb_sem,
):
    toks, gps, dxs, rss = (tok0, tok1), (gp0, gp1), (dx0, dx1), (rs0, rs1)
    row, c = lax.axis_index("row"), lax.axis_index("col")
    core = row % 2
    x = (row // 2) % NX
    y = row // (2 * NX)
    a = x + (y - x) * core
    b = y + (x - y) * core

    def ring(v, step, n):
        return lax.rem(v + step + n, n)

    def chip(a_, b_):
        x_ = a_ + (b_ - a_) * core
        y_ = b_ + (a_ - b_) * core
        return ((y_ * NX + x_) * 2 + core, c)

    z_to = ((row, ring(c, 1, NZ)), (row, ring(c, -1, NZ)))
    a_to = (chip(ring(a, 1, NX), b), chip(ring(a, -1, NX), b))
    b_to = (chip(a, ring(b, 1, NX)), chip(a, ring(b, -1, NX)))
    sibling = (row + 1 - 2 * core, c)

    def remote(src, dst, sends, recv, to):
        return pltpu.make_async_remote_copy(
            src_ref=src, dst_ref=dst, send_sem=send_sem.at[sends], recv_sem=recv, device_id=to, device_id_type=MESH
        )

    def send(src, dst, sends, recv, to):
        remote(src, dst, sends, recv, to).start()

    def landed(region, recv):
        pltpu.make_async_copy(region, region, recv).wait()

    def out(src, dst, at):
        pltpu.make_async_copy(src, dst, out_sem.at[at]).start()

    w_load = pltpu.make_async_copy(w_hbm, wg.at[pl.ds(((core * NX + a) * NX + b) * 6, 6)], load_sem.at[2])
    cot_load = pltpu.make_async_copy(cot_hbm, cot, load_sem.at[3])

    def tok_load(h):
        for i in range(FB):
            pltpu.make_async_copy(
                tok_hbm.at[pl.ds(h * T, T), pl.ds(i * BLK, BLK)], toks[h].at[c * FB + i], load_sem.at[h]
            ).start()

    def tok_wait(h):
        region = toks[h].at[pl.ds(c * FB, FB)]
        pltpu.make_async_copy(region, region, load_sem.at[h]).wait()

    tok_load(0)
    w_load.start()
    pltpu.make_async_copy(cols_hbm, cols, load_sem.at[4]).start()
    pltpu.make_async_copy(cols_hbm, cols_v, load_sem.at[5]).start()
    tok_load(1)
    cot_load.start()

    barrier = pltpu.get_barrier_semaphore()
    for to in (*z_to, *a_to, *b_to, sibling):
        pl.semaphore_signal(barrier, inc=1, device_id=to, device_id_type=MESH)
    pl.semaphore_wait(barrier, 7)

    def ag_region(h, shard, way, step, p):
        rows = pl.ds(0, T) if step < 4 else pl.ds(way * HALF, HALF)
        return toks[h].at[pl.ds(shard * FB + p * (FB // NP), FB // NP), rows]

    def ag_at(way, step):
        return 6 if step == 4 else 2 * (step - 1) + way

    def ag_send(h, way, step, p):
        shard = ring(c, (1 - step) if way == 0 else (step - 1), NZ)
        region = ag_region(h, shard, way, step, p)
        send(region, region, h, ag_sem.at[h, ag_at(way, step), p], z_to[way])

    def ag_event(h, step, p):
        if step == 4:
            landed(ag_region(h, ring(c, 4, NZ), 0, 1, p), ag_sem.at[h, 6, p])
            return
        for way in range(2):
            shard = ring(c, -step if way == 0 else step, NZ)
            landed(ag_region(h, shard, way, step, p), ag_sem.at[h, ag_at(way, step), p])
            ag_send(h, way, step + 1, p)

    def ag_open(h):
        for p in range(NP):
            for way in range(2):
                ag_send(h, way, 1, p)

    def w_region(core_, a_, b_, lo=0, n=6):
        return wg.at[pl.ds(((core_ * NX + a_) * NX + b_) * 6 + lo, n)]

    def b_of(q):
        return ring(b, (0, 1, -1, 2)[q], NX)

    def w_to_a(q):
        region = w_region(core, a, b_of(q))
        for way in range(2):
            send(region, region, 4, wa_sem.at[way, q], a_to[way])

    def w_to_sibling(g, q):
        region = w_region(core, ring(a, (0, 1, -1, 2)[g], NX), b_of(q))
        send(region, region, 4, wc_sem.at[0], sibling)

    def w_open():
        region = w_region(core, a, b)
        for way in range(2):
            send(region, region, 4, wb_sem.at[way], b_to[way])
        w_to_a(0)
        w_to_sibling(0, 0)

    def w_near_b():
        for way in range(2):
            q = 2 if way == 0 else 1
            landed(w_region(core, a, b_of(q)), wb_sem.at[way])
            region = w_region(core, a, b_of(q), 3 * way, 3)
            send(region, region, 4, wb_sem.at[2], b_to[way])
            w_to_a(q)
            w_to_sibling(0, q)

    def w_far_b():
        landed(w_region(core, a, b_of(3)), wb_sem.at[2])
        w_to_a(3)
        w_to_sibling(0, 3)

    def w_near_a(q):
        for way in range(2):
            g = 2 if way == 0 else 1
            a_ = ring(a, -1 if way == 0 else 1, NX)
            landed(w_region(core, a_, b_of(q)), wa_sem.at[way, q])
            region = w_region(core, a_, b_of(q), 3 * way, 3)
            send(region, region, 4, wa_sem.at[2, q], a_to[way])
            w_to_sibling(g, q)

    def w_far_a(q):
        landed(w_region(core, ring(a, 2, NX), b_of(q)), wa_sem.at[2, q])
        w_to_sibling(3, q)

    def w_close():
        landed(wg.at[pl.ds((1 - core) * DB, DB)], wc_sem.at[0])

    def plan_places():
        pltpu.make_async_copy(cols_hbm, cols, load_sem.at[4]).wait()
        pltpu.make_async_copy(cols_hbm, cols_v, load_sem.at[5]).wait()
        mine = cols_v[...]
        order = lax.broadcasted_iota(jnp.int32, (KP, DB), 0) * DB + lax.broadcasted_iota(jnp.int32, (KP, DB), 1)
        lane = lax.broadcasted_iota(jnp.int32, (8, BLK), 1)

        def body(k, carry):
            at, counts = carry
            for s in range(KP):
                col = cols[s, k]
                before = (col < mine) | ((col == mine) & (s * DB + k < order))
                at = at + jnp.where(before, 1, 0)
                counts = counts + jnp.where(lane == col, 1, 0)
            return at, counts

        at, counts = lax.fori_loop(
            0, DB, body, (jnp.zeros((KP, DB), jnp.int32), jnp.zeros((8, BLK), jnp.int32)), unroll=4
        )
        count_v[...] = counts
        copy = pltpu.make_async_copy(count_v, count, load_sem.at[6])
        copy.start()
        copy.wait()
        pair = lane
        keep = jnp.ones((8, BLK), jnp.int32)
        last = jnp.full((8, BLK), -1, jnp.int32)
        base = jnp.int32(0)
        for j in range(PB):
            n = count[0, j]
            pairs = lax.shift_right_logical(n + 1, 1)
            at = at + jnp.where(mine > j, n & 1, 0)
            keep = jnp.where(pair == base, 0, keep)
            last = last + jnp.where(lane >= j, pairs, 0)
            base = base + pairs
        place_v[...] = at
        copy = pltpu.make_async_copy(place_v, place, load_sem.at[6])
        copy.start()
        copy.wait()
        tab_v[pl.ds(8, 8)] = keep
        tab_v[pl.ds(16, 8)] = last

    def plan_table():
        slot = 2 * lax.broadcasted_iota(jnp.int32, (8, BLK), 1) + lax.broadcasted_iota(jnp.int32, (8, BLK), 0)

        def body(k, carry):
            rows, where = carry
            first = weight_position(k)
            for s in range(KP):
                hit = slot == place[s, k]
                rows = jnp.where(hit, k, rows)
                where = jnp.where(hit, first + s, where)
            return rows, where

        rows, where = lax.fori_loop(
            0, DB, body, (jnp.zeros((8, BLK), jnp.int32), jnp.full((8, BLK), ENT, jnp.int32)), unroll=2
        )
        tab_v[pl.ds(0, 8)] = rows
        tab_v[pl.ds(24, 8)] = where
        copy = pltpu.make_async_copy(tab_v, tab, load_sem.at[6])
        copy.start()
        copy.wait()

    def lanes(k):
        return pl.ds(pl.multiple_of(k * BLK, BLK), BLK)

    def fwd(h, lo, hi):
        tok = toks[h]

        def body(i, acc):
            xs = jnp.concatenate([tok[tab[TAB_K + s, i]] for s in range(2)], axis=1)
            ws = jnp.concatenate([wg[tab[TAB_W + s, i]] for s in range(2)], axis=0)
            acc = acc * tab[TAB_KEEP, i].astype(F32) + jnp.dot(xs, ws, preferred_element_type=F32)
            seg[i] = acc
            return acc

        start = jnp.zeros((T, BLK), F32) if lo == 0 else seg[lo - 1]
        lax.fori_loop(lo, hi, body, start, unroll=3)

    def gelu(h):
        rows = pl.ds(h * T, T)

        def body(j, carry):
            v = seg[tab[TAB_LAST, j]]
            k0 = 0.7978845608028654
            v2 = v * v
            th = jnp.tanh(k0 * (v + 0.044715 * (v2 * v)))
            half = 0.5 * (1.0 + th)
            slope = half + (0.5 * v) * (1.0 - th * th) * (k0 * (1.0 + 3 * 0.044715 * v2))
            act[rows, lanes(j)] = (v * half).astype(BF16)
            gps[h][j] = (cot[rows, lanes(j)].astype(F32) * slope).astype(BF16)
            return carry

        lax.fori_loop(0, PB, body, 0)
        out(act.at[rows], act_hbm.at[rows], 0)

    def grad_x(h, shard):
        gp, dx = gps[h], dxs[h]

        def body(i, carry):
            k = shard * FB + i
            at = weight_position(k)
            gs = jnp.concatenate([gp[cols[s, k]] for s in range(2)], axis=1)
            ws = jnp.concatenate([wg[at + s] for s in range(2)], axis=1)
            out = lax.dot_general(gs, ws, (((1,), (1,)), ((), ())), preferred_element_type=F32)
            dx[:, lanes(k)] = out.astype(BF16)
            return carry

        lax.fori_loop(0, FB, body, 0, unroll=3)

    def grad_w(core_, a_):
        def body(i, carry):
            b_, j = i // 3, i % 3
            at = (((core_ * NX + a_) * NX + b_) * 3 + j) * 2
            x_ = a_ + (b_ - a_) * core_
            y_ = b_ + (a_ - b_) * core_
            k = ((y_ * NX + x_) * 2 + core_) * 3 + j
            xs = jnp.concatenate([tok[k] for tok in toks], axis=0)
            picks = [cols[s, k] for s in range(2)]
            gs = jnp.concatenate(
                [jnp.concatenate([gp[col] for gp in gps], axis=0) for col in picks], axis=1
            )
            out = lax.dot_general(xs, gs, (((0,), (0,)), ((), ())), preferred_element_type=F32)
            dw[at] = out[:, :BLK].astype(BF16)
            dw[at + 1] = out[:, BLK:].astype(BF16)
            return carry

        lax.fori_loop(0, 12, body, 0, unroll=2)

    def rs_rows(way, step):
        return pl.ds(0, HALF) if step == 1 else pl.ds(HALF + (step - 2) * T, T)

    def rs_send(h, way, step, p):
        shard = ring(c, (5 - step) if way == 0 else (step - 5), NZ)
        col = pl.ds(pl.multiple_of(shard * FEAT + p * PW, PW), PW)
        rows = pl.ds(way * HALF, HALF) if step == 1 else pl.ds(0, T)
        send(
            dxs[h].at[rows, col],
            rss[h].at[way, rs_rows(way, step), pl.ds(p * PW, PW)],
            2 + h,
            rs_sem.at[h, ag_at(way, step), p],
            z_to[way],
        )

    def rs_open(h):
        for p in range(NP):
            for way in range(2):
                rs_send(h, way, 1, p)

    def rs_wait(h, way, step, p):
        ways = way if step < 4 else pl.ds(0, 2)
        landed(rss[h].at[ways, rs_rows(way, step), pl.ds(p * PW, PW)], rs_sem.at[h, ag_at(way, step), p])

    def rs_event(h, step, p):
        dx, rs = dxs[h], rss[h]
        if step < 4:
            for way in range(2):
                rs_wait(h, way, step, p)
                shard = ring(c, (4 - step) if way == 0 else (step - 4), NZ)
                rows = pl.ds(way * HALF, HALF) if step == 1 else pl.ds(0, T)

                def body(i, carry):
                    at = lanes(shard * FB + p * (PW // BLK) + i)
                    got = rs[way, rs_rows(way, step), lanes(p * (PW // BLK) + i)]
                    dx[rows, at] = (dx[rows, at].astype(F32) + got.astype(F32)).astype(BF16)
                    return carry

                lax.fori_loop(0, PW // BLK, body, 0, unroll=2)
                rs_send(h, way, step + 1, p)
        else:
            rs_wait(h, 0, step, p)

            def body(i, carry):
                at = lanes(c * FB + p * (PW // BLK) + i)
                total = dx[:, at].astype(F32)
                for way in range(2):
                    total += rs[way, rs_rows(way, 4), lanes(p * (PW // BLK) + i)].astype(F32)
                dx[:, at] = total.astype(BF16)
                return carry

            lax.fori_loop(0, PW // BLK, body, 0, unroll=2)
            out(
                dx.at[:, pl.ds(pl.multiple_of(c * FEAT + p * PW, PW), PW)],
                gt_hbm.at[pl.ds(h * T, T), pl.ds(p * PW, PW)],
                1,
            )

    def w_at(a_, b_=0):
        return ((core * NX + a_) * NX + b_) * 6

    def pair_send(a_):
        src = dw.at[pl.ds((((1 - core) * NX + a_) * NX) * 6, 24)]
        send(src, pr.at[pl.ds(a_ * 24, 24)], 5, gc_sem.at[a_], sibling)

    def add_blocks(dst, n, *srcs):
        def body(i, carry):
            total = dw[dst + i].astype(F32)
            for ref, at in srcs:
                total += ref[at + i].astype(F32)
            dw[dst + i] = total.astype(BF16)
            return carry

        lax.fori_loop(0, n, body, 0, unroll=2)

    def pair_add(a_):
        landed(pr.at[pl.ds(a_ * 24, 24)], gc_sem.at[a_])
        add_blocks(w_at(a_), 24, (pr, a_ * 24))

    def part(buf, way, step, size):
        off = way * (size + size // 2) + (0 if step == 0 else size // 2)
        return buf.at[pl.ds(off, size // 2 if step == 0 else size)], off

    def ring_open(buf, far, size, sems, tos):
        for way in range(2):
            dst, _ = part(buf, way, 0, size)
            send(dw.at[pl.ds(far + way * (size // 2), size // 2)], dst, 5, sems.at[way, 0], tos[way])

    def ring_middle(buf, nexts, size, sems, tos):
        for way in range(2):
            got, off = part(buf, way, 0, size)
            landed(got, sems.at[way, 0])
            add_blocks(nexts[way] + way * (size // 2), size // 2, (buf, off))
            dst, _ = part(buf, way, 1, size)
            send(dw.at[pl.ds(nexts[way], size)], dst, 5, sems.at[way, 1], tos[way])

    def ring_close(buf, own, size, sems, tos):
        srcs = []
        for way in range(2):
            got, off = part(buf, way, 1, size)
            landed(got, sems.at[way, 1])
            srcs.append((buf, off))
        add_blocks(own, size, *srcs)

    a_near = (w_at(ring(a, 1, NX)), w_at(ring(a, -1, NX)))
    b_near = (w_at(a, ring(b, 1, NX)), w_at(a, ring(b, -1, NX)))

    wg[ENT] = jnp.zeros((BLK, BLK), BF16)
    tok_wait(0)
    ag_open(0)
    w_load.wait()
    w_open()
    w_near_b()
    w_near_a(0)
    w_far_b()
    ag_event(0, 1, 0)
    w_near_a(1)
    w_near_a(2)
    ag_event(0, 1, 1)
    w_near_a(3)
    w_far_a(0)
    w_far_a(1)
    w_far_a(2)
    ag_event(0, 2, 0)
    w_far_a(3)
    plan_places()
    ag_event(0, 2, 1)
    plan_table()
    ag_event(0, 3, 0)
    tok_wait(1)
    ag_event(0, 3, 1)
    ag_open(1)
    cot_load.wait()
    w_close()
    ag_event(0, 4, 0)
    ag_event(0, 4, 1)

    quarter = PAIRS // 4
    fwd(0, 0, quarter)
    ag_event(1, 1, 0)
    fwd(0, quarter, 2 * quarter)
    ag_event(1, 1, 1)
    fwd(0, 2 * quarter, 3 * quarter)
    fwd(0, 3 * quarter, PAIRS)
    ag_event(1, 2, 0)
    gelu(0)
    grad_x(0, ring(c, 4, NZ))
    ag_event(1, 2, 1)
    grad_x(0, ring(c, 3, NZ))
    grad_x(0, ring(c, -3, NZ))
    grad_x(0, ring(c, 2, NZ))
    ag_event(1, 3, 0)
    grad_x(0, ring(c, -2, NZ))
    grad_x(0, ring(c, 1, NZ))
    grad_x(0, ring(c, -1, NZ))
    grad_x(0, c)
    ag_event(1, 3, 1)
    rs_open(0)
    ag_event(1, 4, 0)
    ag_event(1, 4, 1)

    fwd(1, 0, quarter)
    rs_event(0, 1, 0)
    fwd(1, quarter, 2 * quarter)
    rs_event(0, 1, 1)
    fwd(1, 2 * quarter, 3 * quarter)
    fwd(1, 3 * quarter, PAIRS)
    gelu(1)
    rs_event(0, 2, 0)
    for g in range(2):
        grad_w(1 - core, g)
        pair_send(g)
    rs_event(0, 2, 1)
    for g in range(2, 4):
        grad_w(1 - core, g)
        pair_send(g)
    grad_w(core, ring(a, 2, NX))
    rs_event(0, 3, 0)
    grad_x(1, ring(c, 4, NZ))
    rs_open(1)
    pair_add(ring(a, 2, NX))
    ring_open(bufa, w_at(ring(a, 2, NX)), 24, ga_sem, a_to)
    grad_w(core, ring(a, 1, NX))
    grad_w(core, ring(a, -1, NX))
    rs_event(0, 3, 1)
    grad_x(1, ring(c, 3, NZ))
    grad_x(1, ring(c, -3, NZ))
    pair_add(ring(a, 1, NX))
    pair_add(ring(a, -1, NX))
    ring_middle(bufa, a_near, 24, ga_sem, a_to)
    rs_event(1, 1, 0)
    grad_w(core, a)
    pair_add(a)
    rs_event(0, 4, 0)
    grad_x(1, ring(c, 2, NZ))
    grad_x(1, ring(c, -2, NZ))
    rs_event(1, 1, 1)
    rs_event(0, 4, 1)
    grad_x(1, ring(c, 1, NZ))
    grad_x(1, ring(c, -1, NZ))
    grad_x(1, c)
    rs_event(1, 2, 0)
    ring_close(bufa, w_at(a), 24, ga_sem, a_to)
    ring_open(bufb, w_at(a, ring(b, 2, NX)), 6, gb_sem, b_to)
    rs_event(1, 2, 1)
    ring_middle(bufb, b_near, 6, gb_sem, b_to)
    rs_event(1, 3, 0)
    ring_close(bufb, w_at(a, b), 6, gb_sem, b_to)
    out(dw.at[pl.ds(w_at(a, b), 6)], gb_hbm, 2)
    rs_event(1, 3, 1)
    rs_event(1, 4, 0)
    rs_event(1, 4, 1)

    pltpu.make_async_copy(act, act_hbm, out_sem.at[0]).wait()
    pltpu.make_async_copy(dx0.at[:, pl.ds(0, CHUNKS * FEAT)], dx1.at[:, pl.ds(0, CHUNKS * FEAT)], out_sem.at[1]).wait()
    pltpu.make_async_copy(dw.at[pl.ds(0, 6)], gb_hbm, out_sem.at[2]).wait()
    for h in range(CHUNKS):
        landed(toks[h].at[pl.ds(0, 7 * FB)], send_sem.at[h])
        landed(dxs[h].at[:, pl.ds(0, 7 * FEAT)], send_sem.at[2 + h])
    landed(wg.at[pl.ds(0, 31 * 6)], send_sem.at[4])
    landed(dw.at[pl.ds(0, 31 * 6)], send_sem.at[5])


def finish(act, gt, gb, act_out, gt_out, gb_out, act_v, gt_v, gb_v, sem_in, sem_out):
    parts = [(act, act_v, act_out, pl.ds(i * 64, 64)) for i in range(4)]
    parts += [(gt, gt_v, gt_out, pl.ds(i * 128, 128)) for i in range(2)]
    parts += [(gb, gb_v, gb_out, pl.ds(0, 6))]
    loads = [pltpu.make_async_copy(src.at[at], mid.at[at], sem_in.at[i]) for i, (src, mid, _, at) in enumerate(parts)]
    stores = [pltpu.make_async_copy(mid.at[at], dst.at[at], sem_out.at[i]) for i, (_, mid, dst, at) in enumerate(parts)]
    for copy in loads:
        copy.start()
    for load, store in zip(loads, stores):
        load.wait()
        store.start()
    for copy in stores:
        copy.wait()


def on_device(tokens, weight_blocks, block_cols, cotangent):
    any_space = pl.BlockSpec(memory_space=pl.ANY)
    dma = pltpu.SemaphoreType.DMA
    act, grad_tokens, grad_blocks = pl.pallas_call(
        kernel,
        out_shape=(
            jax.ShapeDtypeStruct((CHUNKS * T, PB * BLK), BF16),
            jax.ShapeDtypeStruct((CHUNKS * T, FEAT), BF16),
            jax.ShapeDtypeStruct((6, BLK, BLK), BF16),
        ),
        in_specs=[any_space] * 4,
        out_specs=(any_space, any_space, any_space),
        scratch_shapes=[
            pltpu.VMEM((DB, T, BLK), BF16),
            pltpu.VMEM((DB, T, BLK), BF16),
            pltpu.VMEM((ENT + 1, BLK, BLK), BF16),
            pltpu.VMEM((PAIRS, T, BLK), F32),
            pltpu.VMEM((CHUNKS * T, PB * BLK), BF16),
            pltpu.VMEM((CHUNKS * T, PB * BLK), BF16),
            pltpu.VMEM((PB, T, BLK), BF16),
            pltpu.VMEM((PB, T, BLK), BF16),
            pltpu.VMEM((T, DB * BLK), BF16),
            pltpu.VMEM((T, DB * BLK), BF16),
            pltpu.VMEM((2, HALF + 3 * T, FEAT), BF16),
            pltpu.VMEM((2, HALF + 3 * T, FEAT), BF16),
            pltpu.VMEM((ENT, BLK, BLK), BF16),
            pltpu.VMEM((ENT // 2, BLK, BLK), BF16),
            pltpu.VMEM((2 * 36, BLK, BLK), BF16),
            pltpu.VMEM((2 * 9, BLK, BLK), BF16),
            pltpu.VMEM((KP, DB), jnp.int32),
            pltpu.SMEM((KP, DB), jnp.int32),
            pltpu.VMEM((8, BLK), jnp.int32),
            pltpu.SMEM((8, BLK), jnp.int32),
            pltpu.VMEM((KP, DB), jnp.int32),
            pltpu.SMEM((KP, DB), jnp.int32),
            pltpu.VMEM((32, BLK), jnp.int32),
            pltpu.SMEM((32, BLK), jnp.int32),
            dma((7,)),
            dma((3,)),
            dma((6,)),
            dma((CHUNKS, 7, NP)),
            dma((CHUNKS, 7, NP)),
            dma((3,)),
            dma((3, 4)),
            dma((1,)),
            dma((4,)),
            dma((2, 2)),
            dma((2, 2)),
        ],
        compiler_params=pltpu.CompilerParams(
            collective_id=0, has_side_effects=True, vmem_limit_bytes=60 * 1024 * 1024
        ),
        cost_estimate=pl.CostEstimate(flops=4_831_838_208, bytes_accessed=6_000_000, transcendentals=786_432),
    )(block_cols.T, tokens, weight_blocks.reshape(6, BLK, BLK), cotangent)
    act, grad_tokens, grad_blocks = pl.pallas_call(
        finish,
        out_shape=tuple(jax.ShapeDtypeStruct(v.shape, v.dtype) for v in (act, grad_tokens, grad_blocks)),
        in_specs=[any_space] * 3,
        out_specs=(any_space,) * 3,
        scratch_shapes=[*(pltpu.VMEM(v.shape, v.dtype) for v in (act, grad_tokens, grad_blocks)), dma((7,)), dma((7,))],
    )(act, grad_tokens, grad_blocks)
    return act, grad_tokens, grad_blocks.reshape(3, KP, BLK, BLK)


def solution(mesh):
    return jax.shard_map(
        on_device,
        mesh=mesh,
        in_specs=(P("row", "col"), P("row", "col", None, None), P(None, "col"), P("row", "col")),
        out_specs=(P("row", "col"), P("row", "col"), P("row", "col", None, None)),
        check_vma=False,
    )
```

time: 157 us -> 135 us (0.86)
  Pallas kernels: 149 us -> 134 us
  local copies, waits for them, and re-layouts: 5.88 us -> 0 us
    pallas_call x1, Pallas kernels: 149 us -> 131 us  [on_device(): pl.pallas_call(kernel, out_shape=(jax.ShapeDtypeStruct((CHUNKS * T, PB *...]
    unnamed x8 -> x0, local copies, waits for them, and re-layouts: 5.08 us -> none
    pallas_call x0 -> x1, Pallas kernels: none -> 2.57 us  [on_device(): pl.pallas_call(finish, out_shape=tuple((jax.ShapeDtypeStruct(v.shape, v.d...]
where the time goes in v2:
time: 135 us; the launch traced here: 134 us
  Pallas kernels  134 us (99%)
    pallas_call x1, Pallas kernels, on_device(): pl.pallas_call(kernel, out_shape=(jax.ShapeDtypeStruct((CHUNKS * T, PB *...  131 us

profile of v2, /device:TPU:2, one launch (start us, length us, event | category | flops | bytes accessed | tf_op | source)
XLA Modules:
  0.0 134.5 jit_solution(7405777093525632897)
XLA Ops:
  0.6 131.3 %shard_map.67 = (bf16[256,3072]{1,0:T(8,128)(2,1)}, bf16[256,1536]{1,0:T(8,128)(2,1)}, bf16[6,128,128]{2,1,0:T(8,128)(2,1)}) custom-call(s32[2,96]{1,0:T(2,128)} %bitcast.5, bf16[256,1536]{1,0:T(8,128)(2,1)} %tok_hbm.1, bf16[6,128,128]{2,1,0:T(8,128)(2,1)} %bitcast.3, bf16[256,3072]{1,0:T(8,128)(2,1)} %cot_hbm.1), custom_call_target="tpu_custom_call" | custom-call | flops 4831838208 | bytes 6000000 | tf_op jit(solution)/shard_map/pallas_call | solution.py:555
  131.9 2.6 %shard_map.68 = (bf16[256,3072]{1,0:T(8,128)(2,1)}, bf16[256,1536]{1,0:T(8,128)(2,1)}, bf16[6,128,128]{2,1,0:T(8,128)(2,1)}) custom-call(bf16[256,3072]{1,0:T(8,128)(2,1)} %get-tuple-element.9.act, bf16[256,1536]{1,0:T(8,128)(2,1)} %get-tuple-element.10.gt, bf16[6,128,128]{2,1,0:T(8,128)(2,1)} %get-tuple-element.11.gb), custom_call_target="tpu_custom_call" | custom-call | tf_op jit(solution)/shard_map/pallas_call | solution.py:606

commit v3 on v2

--- a/solution.py
+++ b/solution.py
@@ -93,16 +93,13 @@
         region = toks[h].at[pl.ds(c * FB, FB)]
         pltpu.make_async_copy(region, region, load_sem.at[h]).wait()
 
+    barrier = pltpu.get_barrier_semaphore()
+    for to in (*z_to, *a_to, *b_to, sibling):
+        pl.semaphore_signal(barrier, inc=1, device_id=to, device_id_type=MESH)
     tok_load(0)
     w_load.start()
     pltpu.make_async_copy(cols_hbm, cols, load_sem.at[4]).start()
     pltpu.make_async_copy(cols_hbm, cols_v, load_sem.at[5]).start()
-    tok_load(1)
-    cot_load.start()
-
-    barrier = pltpu.get_barrier_semaphore()
-    for to in (*z_to, *a_to, *b_to, sibling):
-        pl.semaphore_signal(barrier, inc=1, device_id=to, device_id_type=MESH)
     pl.semaphore_wait(barrier, 7)
 
     def ag_region(h, shard, way, step, p):
@@ -423,18 +420,20 @@
     ag_open(0)
     w_load.wait()
     w_open()
+    tok_load(1)
+    cot_load.start()
     w_near_b()
     w_near_a(0)
+    ag_event(0, 1, 0)
     w_far_b()
-    ag_event(0, 1, 0)
     w_near_a(1)
     w_near_a(2)
     ag_event(0, 1, 1)
     w_near_a(3)
     w_far_a(0)
+    ag_event(0, 2, 0)
     w_far_a(1)
     w_far_a(2)
-    ag_event(0, 2, 0)
     w_far_a(3)
     plan_places()
     ag_event(0, 2, 1)
@@ -534,23 +533,22 @@
     landed(dw.at[pl.ds(0, 31 * 6)], send_sem.at[5])
 
 
-def finish(act, gt, gb, act_out, gt_out, gb_out, act_v, gt_v, gb_v, sem_in, sem_out):
-    parts = [(act, act_v, act_out, pl.ds(i * 64, 64)) for i in range(4)]
-    parts += [(gt, gt_v, gt_out, pl.ds(i * 128, 128)) for i in range(2)]
-    parts += [(gb, gb_v, gb_out, pl.ds(0, 6))]
-    loads = [pltpu.make_async_copy(src.at[at], mid.at[at], sem_in.at[i]) for i, (src, mid, _, at) in enumerate(parts)]
-    stores = [pltpu.make_async_copy(mid.at[at], dst.at[at], sem_out.at[i]) for i, (_, mid, dst, at) in enumerate(parts)]
-    for copy in loads:
+def finish(act, gt, gb, act_out, gt_out, gb_out, sem_out):
+    parts = [(act, act_out, pl.ds(i * 64, 64)) for i in range(4)]
+    parts += [(gt, gt_out, pl.ds(i * 128, 128)) for i in range(2)]
+    parts += [(gb, gb_out, pl.ds(0, 6))]
+    stores = [pltpu.make_async_copy(mid.at[at], dst.at[at], sem_out.at[i]) for i, (mid, dst, at) in enumerate(parts)]
+    for copy in stores:
         copy.start()
-    for load, store in zip(loads, stores):
-        load.wait()
-        store.start()
     for copy in stores:
         copy.wait()
 
 
 def on_device(tokens, weight_blocks, block_cols, cotangent):
     any_space = pl.BlockSpec(memory_space=pl.ANY)
+    hbm = pl.BlockSpec(memory_space=pltpu.HBM)
+    arrays = (block_cols.T, tokens, weight_blocks.reshape(6, BLK, BLK), cotangent)
+    in_hbm = [pltpu.with_memory_space_constraint(v, pltpu.HBM) for v in arrays]
     dma = pltpu.SemaphoreType.DMA
     act, grad_tokens, grad_blocks = pl.pallas_call(
         kernel,
@@ -559,7 +557,7 @@
             jax.ShapeDtypeStruct((CHUNKS * T, FEAT), BF16),
             jax.ShapeDtypeStruct((6, BLK, BLK), BF16),
         ),
-        in_specs=[any_space] * 4,
+        in_specs=[hbm] * 4,
         out_specs=(any_space, any_space, any_space),
         scratch_shapes=[
             pltpu.VMEM((DB, T, BLK), BF16),
@@ -599,16 +597,17 @@
             dma((2, 2)),
         ],
         compiler_params=pltpu.CompilerParams(
-            collective_id=0, has_side_effects=True, vmem_limit_bytes=60 * 1024 * 1024
+            collective_id=0, has_side_effects=True, vmem_limit_bytes=50 * 1024 * 1024
         ),
         cost_estimate=pl.CostEstimate(flops=4_831_838_208, bytes_accessed=6_000_000, transcendentals=786_432),
-    )(block_cols.T, tokens, weight_blocks.reshape(6, BLK, BLK), cotangent)
+    )(*in_hbm)
     act, grad_tokens, grad_blocks = pl.pallas_call(
         finish,
         out_shape=tuple(jax.ShapeDtypeStruct(v.shape, v.dtype) for v in (act, grad_tokens, grad_blocks)),
         in_specs=[any_space] * 3,
-        out_specs=(any_space,) * 3,
-        scratch_shapes=[*(pltpu.VMEM(v.shape, v.dtype) for v in (act, grad_tokens, grad_blocks)), dma((7,)), dma((7,))],
+        out_specs=(hbm,) * 3,
+        scratch_shapes=[dma((7,))],
+        compiler_params=pltpu.CompilerParams(vmem_limit_bytes=1024 * 1024),
     )(act, grad_tokens, grad_blocks)
     return act, grad_tokens, grad_blocks.reshape(3, KP, BLK, BLK)
 

time: 135 us -> 132 us (0.978)
  Pallas kernels: 134 us -> 131 us
    pallas_call x1, Pallas kernels: 131 us -> 130 us  [on_device(): pl.pallas_call(kernel, out_shape=(jax.ShapeDtypeStruct((CHUNKS * T, PB *...]
where the time goes in v3:
time: 132 us
  Pallas kernels  131 us (99%)
    pallas_call x1, Pallas kernels, on_device(): pl.pallas_call(kernel, out_shape=(jax.ShapeDtypeStruct((CHUNKS * T, PB *...  130 us

profile of v3, /device:TPU:2, one launch (start us, length us, event | category | flops | bytes accessed | tf_op | source)
XLA Modules:
  0.0 131.8 jit_solution(13717151014573756110)
XLA Ops:
  0.6 129.7 %shard_map.67 = (bf16[256,3072]{1,0:T(8,128)(2,1)S(1)}, bf16[256,1536]{1,0:T(8,128)(2,1)S(1)}, bf16[6,128,128]{2,1,0:T(8,128)(2,1)S(1)}) custom-call(s32[2,96]{1,0:T(2,128)} %bitcast.5, bf16[256,1536]{1,0:T(8,128)(2,1)} %tok_hbm.1, bf16[6,128,128]{2,1,0:T(8,128)(2,1)} %bitcast.3, bf16[256,3072]{1,0:T(8,128)(2,1)} %cot_hbm.1), custom_call_target="tpu_custom_call" | custom-call | flops 4831838208 | bytes 6000000 | tf_op jit(solution)/shard_map/pallas_call | solution.py:553
  130.3 1.5 %shard_map.68 = (bf16[256,3072]{1,0:T(8,128)(2,1)}, bf16[256,1536]{1,0:T(8,128)(2,1)}, bf16[6,128,128]{2,1,0:T(8,128)(2,1)}) custom-call(bf16[256,3072]{1,0:T(8,128)(2,1)S(1)} %get-tuple-element.9.act, bf16[256,1536]{1,0:T(8,128)(2,1)S(1)} %get-tuple-element.10.gt, bf16[6,128,128]{2,1,0:T(8,128)(2,1)S(1)} %get-tuple-element.11.gb), custom_call_target="tpu_custom_call" | custom-call | tf_op jit(solution)/shard_map/pallas_call | solution.py:604

commit v4 on v3

--- a/solution.py
+++ b/solution.py
@@ -422,26 +422,26 @@
     w_open()
     tok_load(1)
     cot_load.start()
+    ag_event(0, 1, 0)
     w_near_b()
     w_near_a(0)
-    ag_event(0, 1, 0)
+    ag_event(0, 1, 1)
     w_far_b()
+    ag_event(0, 2, 0)
     w_near_a(1)
     w_near_a(2)
-    ag_event(0, 1, 1)
+    ag_event(0, 2, 1)
     w_near_a(3)
     w_far_a(0)
-    ag_event(0, 2, 0)
+    ag_event(0, 3, 0)
     w_far_a(1)
     w_far_a(2)
     w_far_a(3)
-    plan_places()
-    ag_event(0, 2, 1)
-    plan_table()
-    ag_event(0, 3, 0)
     tok_wait(1)
     ag_event(0, 3, 1)
     ag_open(1)
+    plan_places()
+    plan_table()
     cot_load.wait()
     w_close()
     ag_event(0, 4, 0)

time: 132 us -> 131 us (level)
  no operation moved by 1% of the time
where the time goes in v4:
time: 131 us
  Pallas kernels  130 us (99%)
    pallas_call x1, Pallas kernels, on_device(): pl.pallas_call(kernel, out_shape=(jax.ShapeDtypeStruct((CHUNKS * T, PB *...  129 us

profile of v4, /device:TPU:2, one launch (start us, length us, event | category | flops | bytes accessed | tf_op | source)
XLA Modules:
  0.0 130.7 jit_solution(17771816130553759930)
XLA Ops:
  0.6 128.5 %shard_map.67 = (bf16[256,3072]{1,0:T(8,128)(2,1)S(1)}, bf16[256,1536]{1,0:T(8,128)(2,1)S(1)}, bf16[6,128,128]{2,1,0:T(8,128)(2,1)S(1)}) custom-call(s32[2,96]{1,0:T(2,128)} %bitcast.5, bf16[256,1536]{1,0:T(8,128)(2,1)} %tok_hbm.1, bf16[6,128,128]{2,1,0:T(8,128)(2,1)} %bitcast.3, bf16[256,3072]{1,0:T(8,128)(2,1)} %cot_hbm.1), custom_call_target="tpu_custom_call" | custom-call | flops 4831838208 | bytes 6000000 | tf_op jit(solution)/shard_map/pallas_call | solution.py:553
  129.2 1.5 %shard_map.68 = (bf16[256,3072]{1,0:T(8,128)(2,1)}, bf16[256,1536]{1,0:T(8,128)(2,1)}, bf16[6,128,128]{2,1,0:T(8,128)(2,1)}) custom-call(bf16[256,3072]{1,0:T(8,128)(2,1)S(1)} %get-tuple-element.9.act, bf16[256,1536]{1,0:T(8,128)(2,1)S(1)} %get-tuple-element.10.gt, bf16[6,128,128]{2,1,0:T(8,128)(2,1)S(1)} %get-tuple-element.11.gb), custom_call_target="tpu_custom_call" | custom-call | tf_op jit(solution)/shard_map/pallas_call | solution.py:604

commit v5 on v4

--- a/solution.py
+++ b/solution.py
@@ -106,22 +106,17 @@
         rows = pl.ds(0, T) if step < 4 else pl.ds(way * HALF, HALF)
         return toks[h].at[pl.ds(shard * FB + p * (FB // NP), FB // NP), rows]
 
-    def ag_at(way, step):
-        return 6 if step == 4 else 2 * (step - 1) + way
-
     def ag_send(h, way, step, p):
         shard = ring(c, (1 - step) if way == 0 else (step - 1), NZ)
         region = ag_region(h, shard, way, step, p)
-        send(region, region, h, ag_sem.at[h, ag_at(way, step), p], z_to[way])
+        send(region, region, h, ag_sem.at[h, step - 1, p], z_to[way])
 
     def ag_event(h, step, p):
-        if step == 4:
-            landed(ag_region(h, ring(c, 4, NZ), 0, 1, p), ag_sem.at[h, 6, p])
-            return
-        for way in range(2):
-            shard = ring(c, -step if way == 0 else step, NZ)
-            landed(ag_region(h, shard, way, step, p), ag_sem.at[h, ag_at(way, step), p])
-            ag_send(h, way, step + 1, p)
+        n = FB // NP if step == 4 else 2 * FB // NP
+        landed(toks[h].at[pl.ds(0, n)], ag_sem.at[h, step - 1, p])
+        if step < 4:
+            for way in range(2):
+                ag_send(h, way, step + 1, p)
 
     def ag_open(h):
         for p in range(NP):
@@ -319,7 +314,7 @@
             dxs[h].at[rows, col],
             rss[h].at[way, rs_rows(way, step), pl.ds(p * PW, PW)],
             2 + h,
-            rs_sem.at[h, ag_at(way, step), p],
+            rs_sem.at[h, step - 1, p],
             z_to[way],
         )
 
@@ -328,15 +323,14 @@
             for way in range(2):
                 rs_send(h, way, 1, p)
 
-    def rs_wait(h, way, step, p):
-        ways = way if step < 4 else pl.ds(0, 2)
-        landed(rss[h].at[ways, rs_rows(way, step), pl.ds(p * PW, PW)], rs_sem.at[h, ag_at(way, step), p])
+    def rs_wait(h, step, p):
+        landed(rss[h].at[:, rs_rows(0, step), pl.ds(p * PW, PW)], rs_sem.at[h, step - 1, p])
 
     def rs_event(h, step, p):
         dx, rs = dxs[h], rss[h]
+        rs_wait(h, step, p)
         if step < 4:
             for way in range(2):
-                rs_wait(h, way, step, p)
                 shard = ring(c, (4 - step) if way == 0 else (step - 4), NZ)
                 rows = pl.ds(way * HALF, HALF) if step == 1 else pl.ds(0, T)
 
@@ -349,8 +343,6 @@
                 lax.fori_loop(0, PW // BLK, body, 0, unroll=2)
                 rs_send(h, way, step + 1, p)
         else:
-            rs_wait(h, 0, step, p)
-
             def body(i, carry):
                 at = lanes(c * FB + p * (PW // BLK) + i)
                 total = dx[:, at].astype(F32)
@@ -520,17 +512,18 @@
     ring_close(bufb, w_at(a, b), 6, gb_sem, b_to)
     out(dw.at[pl.ds(w_at(a, b), 6)], gb_hbm, 2)
     rs_event(1, 3, 1)
+    pltpu.make_async_copy(act, act_hbm, out_sem.at[0]).wait()
+    for h in range(CHUNKS):
+        landed(toks[h].at[pl.ds(0, 7 * FB)], send_sem.at[h])
+    landed(dx0.at[:, pl.ds(0, 7 * FEAT)], send_sem.at[2])
+    landed(wg.at[pl.ds(0, 31 * 6)], send_sem.at[4])
+    landed(dw.at[pl.ds(0, 31 * 6)], send_sem.at[5])
+    pltpu.make_async_copy(dw.at[pl.ds(0, 6)], gb_hbm, out_sem.at[2]).wait()
     rs_event(1, 4, 0)
     rs_event(1, 4, 1)
 
-    pltpu.make_async_copy(act, act_hbm, out_sem.at[0]).wait()
+    landed(dx1.at[:, pl.ds(0, 7 * FEAT)], send_sem.at[3])
     pltpu.make_async_copy(dx0.at[:, pl.ds(0, CHUNKS * FEAT)], dx1.at[:, pl.ds(0, CHUNKS * FEAT)], out_sem.at[1]).wait()
-    pltpu.make_async_copy(dw.at[pl.ds(0, 6)], gb_hbm, out_sem.at[2]).wait()
-    for h in range(CHUNKS):
-        landed(toks[h].at[pl.ds(0, 7 * FB)], send_sem.at[h])
-        landed(dxs[h].at[:, pl.ds(0, 7 * FEAT)], send_sem.at[2 + h])
-    landed(wg.at[pl.ds(0, 31 * 6)], send_sem.at[4])
-    landed(dw.at[pl.ds(0, 31 * 6)], send_sem.at[5])
 
 
 def finish(act, gt, gb, act_out, gt_out, gb_out, sem_out):
@@ -587,8 +580,8 @@
             dma((7,)),
             dma((3,)),
             dma((6,)),
-            dma((CHUNKS, 7, NP)),
-            dma((CHUNKS, 7, NP)),
+            dma((CHUNKS, 4, NP)),
+            dma((CHUNKS, 4, NP)),
             dma((3,)),
             dma((3, 4)),
             dma((1,)),

time: 131 us -> 131 us (level)
  no operation moved by 1% of the time
where the time goes in v5:
time: 131 us; the launch traced here: 130 us
  Pallas kernels  130 us (99%)
    pallas_call x1, Pallas kernels, on_device(): pl.pallas_call(kernel, out_shape=(jax.ShapeDtypeStruct((CHUNKS * T, PB *...  128 us

profile of v5, /device:TPU:2, one launch (start us, length us, event | category | flops | bytes accessed | tf_op | source)
XLA Modules:
  0.0 130.5 jit_solution(12893153206823730086)
XLA Ops:
  0.6 128.3 %shard_map.67 = (bf16[256,3072]{1,0:T(8,128)(2,1)S(1)}, bf16[256,1536]{1,0:T(8,128)(2,1)S(1)}, bf16[6,128,128]{2,1,0:T(8,128)(2,1)S(1)}) custom-call(s32[2,96]{1,0:T(2,128)} %bitcast.5, bf16[256,1536]{1,0:T(8,128)(2,1)} %tok_hbm.1, bf16[6,128,128]{2,1,0:T(8,128)(2,1)} %bitcast.3, bf16[256,3072]{1,0:T(8,128)(2,1)} %cot_hbm.1), custom_call_target="tpu_custom_call" | custom-call | flops 4831838208 | bytes 6000000 | tf_op jit(solution)/shard_map/pallas_call | solution.py:546
  128.9 1.5 %shard_map.68 = (bf16[256,3072]{1,0:T(8,128)(2,1)}, bf16[256,1536]{1,0:T(8,128)(2,1)}, bf16[6,128,128]{2,1,0:T(8,128)(2,1)}) custom-call(bf16[256,3072]{1,0:T(8,128)(2,1)S(1)} %get-tuple-element.9.act, bf16[256,1536]{1,0:T(8,128)(2,1)S(1)} %get-tuple-element.10.gt, bf16[6,128,128]{2,1,0:T(8,128)(2,1)S(1)} %get-tuple-element.11.gb), custom_call_target="tpu_custom_call" | custom-call | tf_op jit(solution)/shard_map/pallas_call | solution.py:597

commit v6 on v5

--- a/solution.py
+++ b/solution.py
@@ -40,8 +40,8 @@
 
 def kernel(
     cols_hbm, tok_hbm, w_hbm, cot_hbm,
-    act_hbm, gt_hbm, gb_hbm,
-    tok0, tok1, wg, seg, cot, act, gp0, gp1, dx0, dx1, rs0, rs1, dw, pr, bufa, bufb,
+    act, gt, gb,
+    tok0, tok1, wg, seg, cot, gp0, gp1, dx0, dx1, rs0, rs1, dw, pr, bufa, bufb,
     cols_v, cols, count_v, count, place_v, place, tab_v, tab,
     load_sem, out_sem, send_sem, ag_sem, rs_sem, wb_sem, wa_sem, wc_sem, gc_sem, ga_sem, gb_sem,
 ):
@@ -268,7 +268,6 @@
             return carry
 
         lax.fori_loop(0, PB, body, 0)
-        out(act.at[rows], act_hbm.at[rows], 0)
 
     def grad_x(h, shard):
         gp, dx = gps[h], dxs[h]
@@ -348,15 +347,10 @@
                 total = dx[:, at].astype(F32)
                 for way in range(2):
                     total += rs[way, rs_rows(way, 4), lanes(p * (PW // BLK) + i)].astype(F32)
-                dx[:, at] = total.astype(BF16)
+                gt[pl.ds(h * T, T), lanes(p * (PW // BLK) + i)] = total.astype(BF16)
                 return carry
 
             lax.fori_loop(0, PW // BLK, body, 0, unroll=2)
-            out(
-                dx.at[:, pl.ds(pl.multiple_of(c * FEAT + p * PW, PW), PW)],
-                gt_hbm.at[pl.ds(h * T, T), pl.ds(p * PW, PW)],
-                1,
-            )
 
     def w_at(a_, b_=0):
         return ((core * NX + a_) * NX + b_) * 6
@@ -510,20 +504,18 @@
     ring_middle(bufb, b_near, 6, gb_sem, b_to)
     rs_event(1, 3, 0)
     ring_close(bufb, w_at(a, b), 6, gb_sem, b_to)
-    out(dw.at[pl.ds(w_at(a, b), 6)], gb_hbm, 2)
+    out(dw.at[pl.ds(w_at(a, b), 6)], gb, 0)
     rs_event(1, 3, 1)
-    pltpu.make_async_copy(act, act_hbm, out_sem.at[0]).wait()
     for h in range(CHUNKS):
         landed(toks[h].at[pl.ds(0, 7 * FB)], send_sem.at[h])
     landed(dx0.at[:, pl.ds(0, 7 * FEAT)], send_sem.at[2])
     landed(wg.at[pl.ds(0, 31 * 6)], send_sem.at[4])
     landed(dw.at[pl.ds(0, 31 * 6)], send_sem.at[5])
-    pltpu.make_async_copy(dw.at[pl.ds(0, 6)], gb_hbm, out_sem.at[2]).wait()
+    pltpu.make_async_copy(dw.at[pl.ds(0, 6)], gb, out_sem.at[0]).wait()
     rs_event(1, 4, 0)
     rs_event(1, 4, 1)
 
     landed(dx1.at[:, pl.ds(0, 7 * FEAT)], send_sem.at[3])
-    pltpu.make_async_copy(dx0.at[:, pl.ds(0, CHUNKS * FEAT)], dx1.at[:, pl.ds(0, CHUNKS * FEAT)], out_sem.at[1]).wait()
 
 
 def finish(act, gt, gb, act_out, gt_out, gb_out, sem_out):
@@ -538,7 +530,6 @@
 
 
 def on_device(tokens, weight_blocks, block_cols, cotangent):
-    any_space = pl.BlockSpec(memory_space=pl.ANY)
     hbm = pl.BlockSpec(memory_space=pltpu.HBM)
     arrays = (block_cols.T, tokens, weight_blocks.reshape(6, BLK, BLK), cotangent)
     in_hbm = [pltpu.with_memory_space_constraint(v, pltpu.HBM) for v in arrays]
@@ -551,13 +542,12 @@
             jax.ShapeDtypeStruct((6, BLK, BLK), BF16),
         ),
         in_specs=[hbm] * 4,
-        out_specs=(any_space, any_space, any_space),
+        out_specs=(pl.BlockSpec(memory_space=pltpu.VMEM),) * 3,
         scratch_shapes=[
             pltpu.VMEM((DB, T, BLK), BF16),
             pltpu.VMEM((DB, T, BLK), BF16),
             pltpu.VMEM((ENT + 1, BLK, BLK), BF16),
             pltpu.VMEM((PAIRS, T, BLK), F32),
-            pltpu.VMEM((CHUNKS * T, PB * BLK), BF16),
             pltpu.VMEM((CHUNKS * T, PB * BLK), BF16),
             pltpu.VMEM((PB, T, BLK), BF16),
             pltpu.VMEM((PB, T, BLK), BF16),
@@ -578,7 +568,7 @@
             pltpu.VMEM((32, BLK), jnp.int32),
             pltpu.SMEM((32, BLK), jnp.int32),
             dma((7,)),
-            dma((3,)),
+            dma((1,)),
             dma((6,)),
             dma((CHUNKS, 4, NP)),
             dma((CHUNKS, 4, NP)),
@@ -597,10 +587,10 @@
     act, grad_tokens, grad_blocks = pl.pallas_call(
         finish,
         out_shape=tuple(jax.ShapeDtypeStruct(v.shape, v.dtype) for v in (act, grad_tokens, grad_blocks)),
-        in_specs=[any_space] * 3,
+        in_specs=[pl.BlockSpec(memory_space=pltpu.VMEM)] * 3,
         out_specs=(hbm,) * 3,
         scratch_shapes=[dma((7,))],
-        compiler_params=pltpu.CompilerParams(vmem_limit_bytes=1024 * 1024),
+        compiler_params=pltpu.CompilerParams(vmem_limit_bytes=4 * 1024 * 1024),
     )(act, grad_tokens, grad_blocks)
     return act, grad_tokens, grad_blocks.reshape(3, KP, BLK, BLK)
 

time: 131 us -> 130 us (level)
  no operation moved by 1% of the time
where the time goes in v6:
time: 130 us
  Pallas kernels  130 us (100%)
    pallas_call x1, Pallas kernels, on_device(): pl.pallas_call(kernel, out_shape=(jax.ShapeDtypeStruct((CHUNKS * T, PB *...  128 us

profile of v6, /device:TPU:2, one launch (start us, length us, event | category | flops | bytes accessed | tf_op | source)
XLA Modules:
  0.0 130.4 jit_solution(10459235973309369782)
XLA Ops:
  0.6 128.2 %shard_map.67 = (bf16[256,3072]{1,0:T(8,128)(2,1)S(1)}, bf16[256,1536]{1,0:T(8,128)(2,1)S(1)}, bf16[6,128,128]{2,1,0:T(8,128)(2,1)S(1)}) custom-call(s32[2,96]{1,0:T(2,128)} %bitcast.5, bf16[256,1536]{1,0:T(8,128)(2,1)} %tok_hbm.1, bf16[6,128,128]{2,1,0:T(8,128)(2,1)} %bitcast.3, bf16[256,3072]{1,0:T(8,128)(2,1)} %cot_hbm.1), custom_call_target="tpu_custom_call" | custom-call | flops 4831838208 | bytes 6000000 | tf_op jit(solution)/shard_map/pallas_call | solution.py:537
  128.9 1.5 %shard_map.68 = (bf16[256,3072]{1,0:T(8,128)(2,1)}, bf16[256,1536]{1,0:T(8,128)(2,1)}, bf16[6,128,128]{2,1,0:T(8,128)(2,1)}) custom-call(bf16[256,3072]{1,0:T(8,128)(2,1)S(1)} %get-tuple-element.9.act, bf16[256,1536]{1,0:T(8,128)(2,1)S(1)} %get-tuple-element.10.gt, bf16[6,128,128]{2,1,0:T(8,128)(2,1)S(1)} %get-tuple-element.11.gb), custom_call_target="tpu_custom_call" | custom-call | tf_op jit(solution)/shard_map/pallas_call | solution.py:587

commit v7 on v6

--- a/solution.py
+++ b/solution.py
@@ -339,7 +339,7 @@
                     dx[rows, at] = (dx[rows, at].astype(F32) + got.astype(F32)).astype(BF16)
                     return carry
 
-                lax.fori_loop(0, PW // BLK, body, 0, unroll=2)
+                lax.fori_loop(0, PW // BLK, body, 0, unroll=True)
                 rs_send(h, way, step + 1, p)
         else:
             def body(i, carry):
@@ -350,7 +350,7 @@
                 gt[pl.ds(h * T, T), lanes(p * (PW // BLK) + i)] = total.astype(BF16)
                 return carry
 
-            lax.fori_loop(0, PW // BLK, body, 0, unroll=2)
+            lax.fori_loop(0, PW // BLK, body, 0, unroll=True)
 
     def w_at(a_, b_=0):
         return ((core * NX + a_) * NX + b_) * 6

time: 130 us -> 130 us (level)
  no operation moved by 1% of the time
where the time goes in v7:
time: 130 us
  Pallas kernels  130 us (100%)
    pallas_call x1, Pallas kernels, on_device(): pl.pallas_call(kernel, out_shape=(jax.ShapeDtypeStruct((CHUNKS * T, PB *...  128 us

profile of v7, /device:TPU:2, one launch (start us, length us, event | category | flops | bytes accessed | tf_op | source)
XLA Modules:
  0.0 130.4 jit_solution(15095930118963702152)
XLA Ops:
  0.6 128.2 %shard_map.67 = (bf16[256,3072]{1,0:T(8,128)(2,1)S(1)}, bf16[256,1536]{1,0:T(8,128)(2,1)S(1)}, bf16[6,128,128]{2,1,0:T(8,128)(2,1)S(1)}) custom-call(s32[2,96]{1,0:T(2,128)} %bitcast.5, bf16[256,1536]{1,0:T(8,128)(2,1)} %tok_hbm.1, bf16[6,128,128]{2,1,0:T(8,128)(2,1)} %bitcast.3, bf16[256,3072]{1,0:T(8,128)(2,1)} %cot_hbm.1), custom_call_target="tpu_custom_call" | custom-call | flops 4831838208 | bytes 6000000 | tf_op jit(solution)/shard_map/pallas_call | solution.py:537
  128.8 1.5 %shard_map.68 = (bf16[256,3072]{1,0:T(8,128)(2,1)}, bf16[256,1536]{1,0:T(8,128)(2,1)}, bf16[6,128,128]{2,1,0:T(8,128)(2,1)}) custom-call(bf16[256,3072]{1,0:T(8,128)(2,1)S(1)} %get-tuple-element.9.act, bf16[256,1536]{1,0:T(8,128)(2,1)S(1)} %get-tuple-element.10.gt, bf16[6,128,128]{2,1,0:T(8,128)(2,1)S(1)} %get-tuple-element.11.gb), custom_call_target="tpu_custom_call" | custom-call | tf_op jit(solution)/shard_map/pallas_call | solution.py:587
